TPU v7x, 32 devices: a whole 2x2x4 slice. The times are simulated.
32 devices in a mesh: wide: 16 (over z, y, core), narrow: 2 (over x).
Axes of the slice: x: 2, y: 2, z: 4, core: 2. Of those that a mesh axis runs over, the one named last changes fastest.
Arguments:
- tokens: bfloat16 [16384, 768], P(('wide', 'narrow')), may hold values from -6 to 6
- memory: bfloat16 [16384, 768], P(('wide', 'narrow')), may hold values from -6 to 6
- target_segments: int32 [16384], P(('wide', 'narrow')), may hold values from 0 to 3, as said below
- memory_segments: int32 [16384], P(('wide', 'narrow')), may hold values from 0 to 3, as said below
- attention_weights: bfloat16 [8, 768, 768], P(None, ('wide', 'narrow')), may hold values from -1 to 1
- expand_weights: bfloat16 [2, 768, 2048], P(None, ('wide', 'narrow')), may hold values from -0.21875 to 0.21875
- contract_weights: bfloat16 [2048, 768], P(('wide', 'narrow')), may hold values from -0.125 to 0.125
- norm_gains: bfloat16 [3, 768], P(None, ('wide', 'narrow')), may hold values from 0.5 to 1.5
- bucket_table: bfloat16 [32, 12], replicated, may hold values from -4 to 4
- cotangent: bfloat16 [16384, 768], P(('wide', 'narrow')), may hold values from -6 to 6
Outputs:
- output: bfloat16 [16384, 768], P(('wide', 'narrow'))
- input_grad: bfloat16 [16384, 768], P(('wide', 'narrow'))
- memory_grad: bfloat16 [16384, 768], P(('wide', 'narrow'))
- attention_grad: float32 [8, 768, 768], P(None, ('wide', 'narrow'))
- expand_grad: float32 [2, 768, 2048], P(None, ('wide', 'narrow'))
- contract_grad: float32 [2048, 768], P(('wide', 'narrow'))
- gains_grad: float32 [3, 768], P(None, ('wide', 'narrow'))
- bucket_grad: float32 [32, 12], replicated
- attention_rows: float32 [6, 768], P(None, ('wide', 'narrow'))
- attention_columns: float32 [6, 768], replicated
- expand_rows: float32 [2, 768], P(None, ('wide', 'narrow'))
- expand_columns: float32 [2, 2048], replicated
- contract_rows: float32 [2048], P(('wide', 'narrow'))
- contract_columns: float32 [768], replicated
- attention_new: float32 [8, 768, 768], P(None, ('wide', 'narrow'))
- expand_new: float32 [2, 768, 2048], P(None, ('wide', 'narrow'))
- contract_new: float32 [2048, 768], P(('wide', 'narrow'))
- projection_statistics: float32 [2, 2, 768], P(None, None, ('wide', 'narrow'))
Inputs may be any that keep to these rules, and one draw needn't show every extreme that they name: `target_segments`: within each packed row the ids never fall and run from 0 to 3, each on one position or more; the memory of the same row holds the same ids likewise. `memory_segments`: within each packed row the ids never fall and run from 0 to 3, each on one slot or more.
All inputs are finite; a program needn't handle non-finite values.
Results may differ from a plain program's by a relative error of at most 0.02.
The roundings to bfloat16 on the way count: a program that leaves them out, or rounds other values in their place, can miss the bound.
Values may be sent and summed in bfloat16 or wider, within the bound.
No kernel may reach another device: no remote copies, remote signals or barrier semaphores. Data moves between devices by JAX's collectives and lax.ppermute only.
A program may use at most 256 MiB of HBM per device.

v0:
```python
import math

import jax
import jax.numpy as jnp
import numpy as np
from jax import lax
from jax.sharding import PartitionSpec as P

D = 768
HEADS = 12
HEAD_DIM = 64
FF = 2048
BUCKETS = 32
MAX_DIST = 128
TGT_LEN = 512
MEM_LEN = 512


NEG_FILL = -1000000000.0
EPSILON = 1e-06
TINY = 1e-30
STEP_RATE = 0.01


def bucket_onehot(length, bucket_count, far_limit):
    exact_span = bucket_count // 2
    onehot_rows = np.zeros((length, bucket_count), np.float32)
    for distance in range(length):
        if distance < exact_span:
            bucket_id = distance
        else:
            bucket_id = min(
                bucket_count - 1,
                exact_span
                + int(
                    math.log(distance / exact_span)
                    / math.log(far_limit / exact_span)
                    * (bucket_count - exact_span)
                ),
            )
        onehot_rows[distance, bucket_id] = 1.0
    return onehot_rows


def distance_grid(length):
    places = np.arange(length)
    return np.maximum(places[:, None] - places[None, :], 0)


def norm_scale(values, gain_row):
    return (
        values * lax.rsqrt(jnp.mean(values * values, axis=-1, keepdims=True) + EPSILON) * gain_row
    )


def to_low(values):
    return values.astype(jnp.bfloat16)


def matmul(left, right):
    return jnp.dot(left, right, preferred_element_type=jnp.float32)


def matmul_tn(left, right):
    return lax.dot_general(
        left, right, (((0,), (0,)), ((), ())), preferred_element_type=jnp.float32
    )


def matmul_nt(left, right):
    return lax.dot_general(
        left, right, (((1,), (1,)), ((), ())), preferred_element_type=jnp.float32
    )


def split_heads(rows, length):
    return rows.reshape(rows.shape[0] // length, length, HEADS, HEAD_DIM)


def self_mask(segment_row):
    causal = jnp.tril(jnp.ones((segment_row.shape[0], segment_row.shape[0]), jnp.bool_))
    return (segment_row[:, None] == segment_row[None, :]) & causal


def cross_mask(segment_row, memory_row):
    return segment_row[:, None] == memory_row[None, :]


def score_grid(query_rows, key_rows, keep_mask, score_bias):
    scores = (
        jnp.einsum("qhd,khd->hqk", query_rows, key_rows, preferred_element_type=jnp.float32)
        + score_bias
    )
    return jnp.where(keep_mask[None], scores, NEG_FILL)


def attend_forward(query_rows, key_rows, value_rows, keep_mask, score_bias):
    scores = score_grid(query_rows, key_rows, keep_mask, score_bias)
    log_total = jax.nn.logsumexp(scores, axis=-1, keepdims=True)
    weights = to_low(jnp.exp(scores - log_total))
    context = jnp.einsum("hqk,khd->qhd", weights, value_rows, preferred_element_type=jnp.float32)
    return (to_low(context), log_total)


def attend_backward(
    query_rows, key_rows, value_rows, keep_mask, score_bias, log_total, context_grad
):
    scores = score_grid(query_rows, key_rows, keep_mask, score_bias)
    probs = jnp.exp(scores - log_total)
    prob_grad = jnp.einsum(
        "qhd,khd->hqk", context_grad, value_rows, preferred_element_type=jnp.float32
    )
    value_grad = jnp.einsum(
        "hqk,qhd->khd", to_low(probs), context_grad, preferred_element_type=jnp.float32
    )
    score_grad = to_low(probs * (prob_grad - jnp.sum(probs * prob_grad, axis=-1, keepdims=True)))
    query_grad = jnp.einsum(
        "hqk,khd->qhd", score_grad, key_rows, preferred_element_type=jnp.float32
    )
    key_grad = jnp.einsum(
        "hqk,qhd->khd", score_grad, query_rows, preferred_element_type=jnp.float32
    )
    return (query_grad, key_grad, value_grad, score_grad)


def forward_pass(tokens, memory, target_rows, memory_rows, score_bias, gathered):
    attention_full, expand_full, contract_full, gains_full = gathered
    gain_rows = gains_full.astype(jnp.float32)
    token_rows = tokens.astype(jnp.float32)
    normed_one = to_low(norm_scale(token_rows, gain_rows[0]))
    query_self = to_low(matmul(normed_one, attention_full[0]))
    key_self = to_low(matmul(normed_one, attention_full[1]))
    value_self = to_low(matmul(normed_one, attention_full[2]))

    def self_step(pack):
        return attend_forward(pack[0], pack[1], pack[2], self_mask(pack[3]), score_bias)

    context_self, total_self = lax.map(
        self_step,
        (
            split_heads(query_self, TGT_LEN),
            split_heads(key_self, TGT_LEN),
            split_heads(value_self, TGT_LEN),
            target_rows,
        ),
    )
    context_self = context_self.reshape(token_rows.shape)
    residual_one = token_rows + matmul(context_self, attention_full[3])
    normed_two = to_low(norm_scale(residual_one, gain_rows[1]))
    query_cross = to_low(matmul(normed_two, attention_full[4]))
    key_cross = to_low(matmul(memory, attention_full[5]))
    value_cross = to_low(matmul(memory, attention_full[6]))

    def cross_step(pack):
        return attend_forward(pack[0], pack[1], pack[2], cross_mask(pack[3], pack[4]), 0.0)

    context_cross, total_cross = lax.map(
        cross_step,
        (
            split_heads(query_cross, TGT_LEN),
            split_heads(key_cross, MEM_LEN),
            split_heads(value_cross, MEM_LEN),
            target_rows,
            memory_rows,
        ),
    )
    context_cross = context_cross.reshape(token_rows.shape)
    residual_two = residual_one + matmul(context_cross, attention_full[7])
    normed_three = to_low(norm_scale(residual_two, gain_rows[2]))
    gate_input = matmul(normed_three, expand_full[0])
    lift_input = matmul(normed_three, expand_full[1])
    hidden = to_low(jax.nn.gelu(gate_input, approximate=True) * lift_input)
    output = residual_two + matmul(hidden, contract_full)
    return (
        gain_rows,
        normed_one,
        query_self,
        key_self,
        value_self,
        context_self,
        total_self,
        residual_one,
        normed_two,
        query_cross,
        key_cross,
        value_cross,
        context_cross,
        total_cross,
        residual_two,
        normed_three,
        gate_input,
        lift_input,
        hidden,
        output,
    )


def factored_stats(grad_shard, total_rows):
    squares = grad_shard * grad_shard + TINY
    return (jnp.mean(squares, axis=-1), jnp.sum(squares, axis=-2) / total_rows)


def factored_update(weight_shard, grad_shard, row_stat, column_stat):
    scale = jnp.mean(column_stat, axis=-1, keepdims=True)[..., None]
    second = row_stat[..., :, None] * column_stat[..., None, :] / scale
    return weight_shard.astype(jnp.float32) - STEP_RATE * grad_shard * lax.rsqrt(second)


def without_outputs(stats):
    return jnp.concatenate([stats[0:3], stats[4:7]], axis=0)


def output_pair(stats):
    return jnp.stack([stats[3], stats[7]])


def on_device(
    tokens,
    memory,
    target_segments,
    memory_segments,
    attention_weights,
    expand_weights,
    contract_weights,
    norm_gains,
    bucket_table,
    cotangent,
):
    row_count = tokens.shape[0]
    memory_count = memory.shape[0]
    target_rows = target_segments.reshape(row_count // TGT_LEN, TGT_LEN)
    memory_rows = memory_segments.reshape(memory_count // MEM_LEN, MEM_LEN)
    onehot_np = bucket_onehot(TGT_LEN, BUCKETS, MAX_DIST)
    pair_buckets = jnp.asarray(onehot_np[distance_grid(TGT_LEN)], jnp.bfloat16)
    score_bias = jnp.einsum(
        "ijb,bh->hij", pair_buckets, bucket_table, preferred_element_type=jnp.float32
    )
    gathered = (
        lax.all_gather(attention_weights, ("wide", "narrow"), axis=1, tiled=True),
        lax.all_gather(expand_weights, ("wide", "narrow"), axis=1, tiled=True),
        lax.all_gather(contract_weights, ("wide", "narrow"), axis=0, tiled=True),
        lax.all_gather(norm_gains, ("wide", "narrow"), axis=1, tiled=True),
    )
    saved = forward_pass(tokens, memory, target_rows, memory_rows, score_bias, gathered)
    output = saved[19].astype(jnp.bfloat16)
    attention_full, expand_full, contract_full, gains_full = gathered
    (
        gain_rows,
        normed_one,
        query_self,
        key_self,
        value_self,
        context_self,
        total_self,
        residual_one,
        normed_two,
        query_cross,
        key_cross,
        value_cross,
        context_cross,
        total_cross,
        residual_two,
        normed_three,
        gate_input,
        lift_input,
        hidden,
        final_rows,
    ) = saved
    contract_full_grad = matmul_tn(hidden, cotangent)
    hidden_grad = matmul_nt(cotangent, contract_full)
    _, gelu_back = jax.vjp(
        lambda gate_in, lift_in: jax.nn.gelu(gate_in, approximate=True) * lift_in,
        gate_input,
        lift_input,
    )
    gate_grad, lift_grad = gelu_back(hidden_grad)
    gate_low = to_low(gate_grad)
    lift_low = to_low(lift_grad)
    expand_full_grad = jnp.stack(
        [matmul_tn(normed_three, gate_low), matmul_tn(normed_three, lift_low)]
    )
    normed_three_grad = matmul_nt(gate_low, expand_full[0]) + matmul_nt(lift_low, expand_full[1])
    _, third_back = jax.vjp(norm_scale, residual_two, gain_rows[2])
    from_third, gain_three_grad = third_back(normed_three_grad)
    residual_two_grad = cotangent.astype(jnp.float32) + from_third
    cross_low = to_low(residual_two_grad)
    cross_out_grad = matmul_tn(context_cross, cross_low)
    context_cross_grad = to_low(matmul_nt(cross_low, attention_full[7]))

    def cross_back(pack):
        found = attend_backward(
            pack[0], pack[1], pack[2], cross_mask(pack[3], pack[4]), 0.0, pack[5], pack[6]
        )
        return (found[0], found[1], found[2])

    cross_query_part, cross_key_part, cross_value_part = lax.map(
        cross_back,
        (
            split_heads(query_cross, TGT_LEN),
            split_heads(key_cross, MEM_LEN),
            split_heads(value_cross, MEM_LEN),
            target_rows,
            memory_rows,
            total_cross,
            split_heads(context_cross_grad, TGT_LEN),
        ),
    )
    cross_query_low = to_low(cross_query_part.reshape(row_count, D))
    cross_key_low = to_low(cross_key_part.reshape(memory_count, D))
    cross_value_low = to_low(cross_value_part.reshape(memory_count, D))
    cross_query_grad = matmul_tn(normed_two, cross_query_low)
    cross_key_grad = matmul_tn(memory, cross_key_low)
    cross_value_grad = matmul_tn(memory, cross_value_low)
    memory_grad = to_low(
        matmul_nt(cross_key_low, attention_full[5]) + matmul_nt(cross_value_low, attention_full[6])
    )
    normed_two_grad = matmul_nt(cross_query_low, attention_full[4])
    _, second_back = jax.vjp(norm_scale, residual_one, gain_rows[1])
    from_second, gain_two_grad = second_back(normed_two_grad)
    residual_one_grad = residual_two_grad + from_second
    self_low = to_low(residual_one_grad)
    self_out_grad = matmul_tn(context_self, self_low)
    context_self_grad = to_low(matmul_nt(self_low, attention_full[3]))

    def self_back(pack):
        found = attend_backward(
            pack[0], pack[1], pack[2], self_mask(pack[3]), score_bias, pack[4], pack[5]
        )
        bucket_sums = jnp.einsum(
            "hqk,qkb->bh", found[3], pair_buckets, preferred_element_type=jnp.float32
        )
        return (found[0], found[1], found[2], bucket_sums)

    self_query_part, self_key_part, self_value_part, bucket_parts = lax.map(
        self_back,
        (
            split_heads(query_self, TGT_LEN),
            split_heads(key_self, TGT_LEN),
            split_heads(value_self, TGT_LEN),
            target_rows,
            total_self,
            split_heads(context_self_grad, TGT_LEN),
        ),
    )
    self_query_low = to_low(self_query_part.reshape(row_count, D))
    self_key_low = to_low(self_key_part.reshape(row_count, D))
    self_value_low = to_low(self_value_part.reshape(row_count, D))
    bucket_part = jnp.sum(bucket_parts, axis=0)
    self_query_grad = matmul_tn(normed_one, self_query_low)
    self_key_grad = matmul_tn(normed_one, self_key_low)
    self_value_grad = matmul_tn(normed_one, self_value_low)
    normed_one_grad = (
        matmul_nt(self_query_low, attention_full[0])
        + matmul_nt(self_key_low, attention_full[1])
        + matmul_nt(self_value_low, attention_full[2])
    )
    _, first_back = jax.vjp(norm_scale, tokens.astype(jnp.float32), gain_rows[0])
    from_first, gain_one_grad = first_back(normed_one_grad)
    input_grad = to_low(residual_one_grad + from_first)
    attention_full_grad = jnp.stack(
        [
            self_query_grad,
            self_key_grad,
            self_value_grad,
            self_out_grad,
            cross_query_grad,
            cross_key_grad,
            cross_value_grad,
            cross_out_grad,
        ]
    )
    gains_full_grad = jnp.stack([gain_one_grad, gain_two_grad, gain_three_grad])
    attention_grad, expand_grad, contract_grad, gains_grad = (
        lax.psum_scatter(attention_full_grad, ("wide", "narrow"), scatter_dimension=1, tiled=True),
        lax.psum_scatter(expand_full_grad, ("wide", "narrow"), scatter_dimension=1, tiled=True),
        lax.psum_scatter(contract_full_grad, ("wide", "narrow"), scatter_dimension=0, tiled=True),
        lax.psum_scatter(gains_full_grad, ("wide", "narrow"), scatter_dimension=1, tiled=True),
    )
    attention_rows, attention_part = factored_stats(attention_grad, D)
    expand_rows, expand_part = factored_stats(expand_grad, D)
    contract_rows, contract_part = factored_stats(contract_grad, FF)
    attention_columns, expand_columns, contract_columns, bucket_grad = lax.psum(
        (attention_part, expand_part, contract_part, bucket_part), ("wide", "narrow")
    )
    attention_new = factored_update(
        attention_weights, attention_grad, attention_rows, attention_columns
    )
    expand_new = factored_update(expand_weights, expand_grad, expand_rows, expand_columns)
    contract_new = factored_update(contract_weights, contract_grad, contract_rows, contract_columns)
    share_width = attention_rows.shape[1]
    share_start = lax.axis_index(("wide", "narrow")) * share_width
    column_share = lax.dynamic_slice_in_dim(attention_columns, share_start, share_width, 1)
    projection_statistics = jnp.stack([output_pair(attention_rows), output_pair(column_share)])
    return (
        output,
        input_grad,
        memory_grad,
        attention_grad,
        expand_grad,
        contract_grad,
        gains_grad,
        bucket_grad,
        without_outputs(attention_rows),
        without_outputs(attention_columns),
        expand_rows,
        expand_columns,
        contract_rows,
        contract_columns,
        attention_new,
        expand_new,
        contract_new,
        projection_statistics,
    )


def solution(mesh):
    placed = (
        P(("wide", "narrow"), None),
        P(("wide", "narrow"), None),
        P(("wide", "narrow")),
        P(("wide", "narrow")),
        P(None, ("wide", "narrow"), None),
        P(None, ("wide", "narrow"), None),
        P(("wide", "narrow"), None),
        P(None, ("wide", "narrow")),
        P(),
        P(("wide", "narrow"), None),
    )
    return jax.shard_map(
        on_device,
        mesh=mesh,
        in_specs=placed,
        out_specs=(
            P(("wide", "narrow"), None),
            P(("wide", "narrow"), None),
            P(("wide", "narrow"), None),
            P(None, ("wide", "narrow"), None),
            P(None, ("wide", "narrow"), None),
            P(("wide", "narrow"), None),
            P(None, ("wide", "narrow")),
            P(),
            P(None, ("wide", "narrow")),
            P(),
            P(None, ("wide", "narrow")),
            P(),
            P(("wide", "narrow")),
            P(),
            P(None, ("wide", "narrow"), None),
            P(None, ("wide", "narrow"), None),
            P(("wide", "narrow"), None),
            P(None, None, ("wide", "narrow")),
        ),
        check_vma=False,
    )
```

profile of v0, /device:TPU:0, one launch (start us, length us, event | category | flops | bytes accessed | tf_op | source)
XLA Modules:
  0.0 786.9 jit_solution(6389110260629920227)
XLA Ops:
  11.4 70.5 %all-gather = bf16[32,24,3]{1,2,0:T(4,128)(2,1)S(1)} all-gather(bf16[1,24,3]{1,2,0:T(4,128)(2,1)} %bitcast.229), channel_id=1, replica_groups=mesh['wide'=16,'narrow'=2] {'wide','narrow'}, dimensions={0}, use_global_device_ids=true | all-gather | bytes 4752 | tf_op jit(solution)/shard_map/all_gather | solution.py:242
  82.3 15.1 %fusion.52 = f32[512,512,12]{1,2,0:T(8,128)} fusion(bf16[512,512,32]{1,2,0:T(8,128)(2,1)} %constant.167.clone, bf16[32,12]{0,1:T(8,128)(2,1)} %param.19), kind=kOutput, calls=%fused_computation.132 | convolution fusion | flops 201326592 | bytes 29360896 | tf_op jit(solution)/shard_map/ijb,bh->hij/dot_general | solution.py:235
  97.3 17.8 %copy.106 = f32[512,512,12]{0,1,2:T(8,128)} copy(f32[512,512,12]{1,2,0:T(8,128)} %fusion.52) | data formatting | bytes 25165824 | tf_op jit(solution)/shard_map/ijb,bh->hij/dot_general | solution.py:235
  123.3 6.6 fusion.69
  147.8 6.7 fusion.29
  170.8 4.0 convolution_convert_fusion.13
  180.2 6.0 fusion.13
  190.0 37.4 %all-gather.9.cloned.1.call-done = bf16[2048,768]{1,0:T(8,128)(2,1)} async-done(((bf16[64,768]{1,0:T(8,128)(2,1)}), bf16[2048,768]{1,0:T(8,128)(2,1)}) %all-gather.9.cloned.1.call-update) | async-done | bytes 3145744 | tf_op jit(solution)/shard_map/all_gather | solution.py:241
  227.4 9.7 %multiply_convert_fusion.2 = (bf16[512,2048]{1,0:T(8,128)(2,1)}, bf16[512,2048]{1,0:T(8,128)(2,1)}, bf16[512,2048]{1,0:T(8,128)(2,1)S(1)}) fusion(f32[512,2048]{1,0:T(8,128)} %fusion.11, f32[512,2048]{1,0:T(8,128)} %fusion.13, bf16[512,768]{1,0:T(8,128)(2,1)} %param.20, bf16[2048,768]{1,0:T(8,128)(2,1)} %all-gather.9.cloned.1.call-done), kind=kOutput, calls=%fused_computation.23 | convolution fusion | flops 1637875712 | bytes 18612224 | tf_op jit(solution)/shard_map/dot_general | solution.py:71
  238.4 4.5 fusion.70
  243.4 6.4 convolution_bitcast_fusion
  249.8 4.4 convolution_bitcast_fusion.1
  254.3 11.8 %pad_maximum_fusion = f32[2,768,2048]{2,1,0:T(8,128)} fusion(f32[1,768,2048]{2,1,0:T(8,128)} %convolution_bitcast_fusion, f32[1,768,2048]{2,1,0:T(8,128)} %convolution_bitcast_fusion.1), kind=kLoop, calls=%fused_computation | loop fusion | flops 3145728 | bytes 25165824 | tf_op jit(solution)/shard_map/stack | solution.py:279
  266.1 4.7 fusion.10
  270.9 4.2 multiply_reduce_fusion.2
  282.0 13.9 %multiply_reduce_fusion.1 = (f32[12,512]{1,0:T(8,128)S(1)}, f32[12,512,512]{1,2,0:T(8,128)}) fusion(f32[12,512,512]{1,2,0:T(8,128)} %copy-done.2, f32[12,512]{1,0:T(8,128)S(1)} %log_add_fusion, pred[512,512]{0,1:T(8,128)(4,1)S(1)} %get-tuple-element.169, bf16[512,12,64]{0,2,1:T(8,128)(2,1)} %bitcast.214, bf16[512,12,64]{0,2,1:T(8,128)(2,1)} %bitcast.213), kind=kOutput, calls=%fused_computation.6 | convolution fusion | flops 415229952 | bytes 27049984 | tf_op jit(solution)/shard_map/while/body/eval_jaxpr/qhd,khd->hqk/dot_general | solution.py:110
  296.0 7.2 multiply_convert_fusion.1
  315.4 12.4 %multiply_reduce_fusion = (f32[12,512]{1,0:T(8,128)S(1)}, f32[12,512,512]{1,2,0:T(8,128)}) fusion(f32[12,512,512]{1,2,0:T(8,128)} %copy-done.1, f32[12,512]{1,0:T(8,128)S(1)} %log_add_fusion.1, bf16[512,12,64]{0,2,1:T(8,128)(2,1)} %bitcast.202, bf16[512,12,64]{0,2,1:T(8,128)(2,1)} %bitcast.201), kind=kOutput, calls=%fused_computation.4 | convolution fusion | flops 412084224 | bytes 26787840 | tf_op jit(solution)/shard_map/while/body/eval_jaxpr/qhd,khd->hqk/dot_general | solution.py:110
  327.8 7.2 multiply_convert_fusion
  365.7 14.8 %copy.122 = bf16[12,512,512]{2,0,1:T(8,128)(2,1)} copy(bf16[12,512,512]{1,2,0:T(8,128)(2,1)} %copy-done.3) | data formatting | bytes 12582912 | tf_op jit(solution)/shard_map/while/body/eval_jaxpr/convert_element_type | solution.py:57
  399.5 7.0 convolution_bitcast_fusion.2
  407.7 111.3 %reduce-scatter.7.cloned.1.call-done = f32[2,24,2048]{2,1,0:T(8,128)} async-done(((f32[2,768,2048]{2,1,0:T(8,128)}), f32[2,24,2048]{2,1,0:T(8,128)}) %reduce-scatter.7.cloned.1.call-update) | async-done | bytes 393232 | tf_op jit(solution)/shard_map/reduce_scatter | solution.py:375
  520.3 209.7 %reduce-scatter.5.cloned.1.call-done = f32[8,24,768]{2,1,0:T(8,128)} async-done(((f32[8,768,768]{2,1,0:T(8,128)}), f32[8,24,768]{2,1,0:T(8,128)}) %reduce-scatter.5.cloned.1.call-update) | async-done | bytes 589840 | tf_op jit(solution)/shard_map/reduce_scatter | solution.py:374
  731.3 40.4 %all-reduce.1 = (f32[3,768]{1,0:T(4,128)S(1)}, f32[32,12]{0,1:T(8,128)}, f32[8,768]{1,0:T(8,128)S(1)}, f32[2,2048]{1,0:T(2,128)S(1)}, f32[768]{0:T(1024)S(1)}) all-reduce(f32[3,768]{1,0:T(4,128)S(1)} %pad_maximum_fusion.2, f32[32,12]{0,1:T(8,128)S(1)} %convolution_bitcast_fusion.2, ...), channel_id=5, replica_groups=mesh['wide'=16,'narrow'=2] {'wide','narrow'}, use_global_device_ids=true, to_apply=%region_18.19.clone | all-reduce | flops 13696 | bytes 109568
  (267 shorter events, 137.1 us)
Async XLA Ops:
  7.2 130.2 %copy-start = (bf16[512,768]{1,0:T(8,128)(2,1)S(1)}, bf16[512,768]{1,0:T(8,128)(2,1)}, u32[]{:S(2)}) copy-start(bf16[512,768]{1,0:T(8,128)(2,1)} %param.12) | copy-start | bytes 2359300
  7.2 109.0 %all-gather.5.cloned.1.call-start = ((), (), s32[]{:S(2)}) async-start(), calls=%async_computation.3 | async-start | bytes 9732096 | tf_op jit(solution)/shard_map/all_gather | solution.py:239
  7.9 172.2 %all-gather.7.cloned.1.call-start = ((), (), s32[]{:S(2)}) async-start(), calls=%async_computation.4 | async-start | bytes 6488064 | tf_op jit(solution)/shard_map/all_gather | solution.py:240
  8.7 218.7 %all-gather.9.cloned.1.call-start = ((), (), s32[]{:S(2)}) async-start(), calls=%async_computation.5 | async-start | bytes 3244032 | tf_op jit(solution)/shard_map/all_gather | solution.py:241
  9.4 397.1 %reduce-scatter.9.cloned.1.call-start = ((), (), s32[]{:S(2)}) async-start(), calls=%async_computation.8 | async-start | bytes 6488064 | tf_op jit(solution)/shard_map/reduce_scatter | solution.py:376
  97.3 17.8 %copy-start.55 = (s32[512]{0:T(512)S(1)}, s32[512]{0:T(512)}, u32[]{:S(2)}) copy-start(s32[512]{0:T(512)} %param.13) | copy-start | bytes 6148
  97.3 17.8 %copy-start.57 = (s32[512]{0:T(512)S(1)}, s32[512]{0:T(512)}, u32[]{:S(2)}) copy-start(s32[512]{0:T(512)} %param.14) | copy-start | bytes 6148
  97.3 18.9 %copy-start.5 = (bf16[512,768]{1,0:T(8,128)(2,1)S(1)}, bf16[512,768]{1,0:T(8,128)(2,1)}, u32[]{:S(2)}) copy-start(bf16[512,768]{1,0:T(8,128)(2,1)} %param.11) | copy-start | bytes 2359300
  243.0 276.1 %reduce-scatter.7.cloned.1.call-start = ((), (), s32[]{:S(2)}) async-start(), calls=%async_computation.7 | async-start | bytes 12976128 | tf_op jit(solution)/shard_map/reduce_scatter | solution.py:375
  266.1 464.0 %reduce-scatter.5.cloned.1.call-start = ((), (), s32[]{:S(2)}) async-start(), calls=%async_computation.6 | async-start | bytes 19464192 | tf_op jit(solution)/shard_map/reduce_scatter | solution.py:374
  282.0 14.0 %slice-start.3 = ((s8[12582912]{0:T(1024)(128)(4,1)}), s8[4194304]{0:T(1024)(128)(4,1)S(1)}, s32[]{:S(2)}) async-start(s8[12582912]{0:T(1024)(128)(4,1)} %bitcast.188), calls=%async_computation.12 | async-start | bytes 8388608
  282.0 14.0 %slice-start.4 = ((s8[12582912]{0:T(1024)(128)(4,1)}), s8[4194304]{0:T(1024)(128)(4,1)S(1)}, s32[]{:S(2)}) async-start(s8[12582912]{0:T(1024)(128)(4,1)} %bitcast.188), calls=%async_computation.13 | async-start | bytes 8388608
  282.0 14.0 %slice-start.5 = ((s8[12582912]{0:T(1024)(128)(4,1)}), s8[4194304]{0:T(1024)(128)(4,1)S(1)}, s32[]{:S(2)}) async-start(s8[12582912]{0:T(1024)(128)(4,1)} %bitcast.188), calls=%async_computation.14 | async-start | bytes 8388608
  315.4 12.4 %slice-start.1 = ((s8[12582912]{0:T(1024)(128)(4,1)}), s8[4194304]{0:T(1024)(128)(4,1)S(1)}, s32[]{:S(2)}) async-start(s8[12582912]{0:T(1024)(128)(4,1)} %bitcast.186), calls=%async_computation.10 | async-start | bytes 8388608
  315.4 12.4 %slice-start.2 = ((s8[12582912]{0:T(1024)(128)(4,1)}), s8[4194304]{0:T(1024)(128)(4,1)S(1)}, s32[]{:S(2)}) async-start(s8[12582912]{0:T(1024)(128)(4,1)} %bitcast.186), calls=%async_computation.11 | async-start | bytes 8388608
  365.7 14.8 %copy-start.41 = (bf16[12,64,512]{2,1,0:T(8,128)(2,1)S(1)}, bf16[12,64,512]{2,1,0:T(8,128)(2,1)}, u32[]{:S(2)}) copy-start(bf16[12,64,512]{2,1,0:T(8,128)(2,1)} %copy-done.40) | copy-start | bytes 2359300
  385.0 13.7 %slice-start.9 = ((s8[16777216]{0:T(1024)(128)(4,1)}), s8[4194304]{0:T(1024)(128)(4,1)S(1)}, s32[]{:S(2)}) async-start(s8[16777216]{0:T(1024)(128)(4,1)} %bitcast.192), calls=%async_computation.18 | async-start | bytes 8388608
  399.5 376.3 %copy-start.45 = (bf16[8,24,768]{2,1,0:T(8,128)(2,1)S(1)}, bf16[8,24,768]{2,1,0:T(8,128)(2,1)}, u32[]{:S(2)}) copy-start(bf16[8,24,768]{2,1,0:T(8,128)(2,1)} %param.15) | copy-start | bytes 884740
  406.5 371.4 %copy-start.50 = (bf16[64,768]{1,0:T(8,128)(2,1)S(1)}, bf16[64,768]{1,0:T(8,128)(2,1)}, u32[]{:S(2)}) copy-start(bf16[64,768]{1,0:T(8,128)(2,1)} %param.17) | copy-start | bytes 294916
  406.5 372.2 %copy-start.46 = (bf16[2,24,2048]{2,1,0:T(8,128)(2,1)S(1)}, bf16[2,24,2048]{2,1,0:T(8,128)(2,1)}, u32[]{:S(2)}) copy-start(bf16[2,24,2048]{2,1,0:T(8,128)(2,1)} %param.16) | copy-start | bytes 589828
  406.5 371.4 %copy-start.47 = (f32[64,768]{1,0:T(8,128)S(1)}, f32[64,768]{1,0:T(8,128)}, u32[]{:S(2)}) copy-start(f32[64,768]{1,0:T(8,128)} %reduce-scatter.9.cloned.1.call-done) | copy-start | bytes 589828
  407.7 371.9 %copy-start.58 = (f32[64]{0:T(128)}, f32[64]{0:T(128)S(1)}, u32[]{:S(2)}) copy-start(f32[64]{0:T(128)S(1)} %broadcast_multiply_fusion.7) | copy-start | bytes 772
  519.1 259.6 %copy-start.44 = (f32[2,24,2048]{2,1,0:T(8,128)S(1)}, f32[2,24,2048]{2,1,0:T(8,128)}, u32[]{:S(2)}) copy-start(f32[2,24,2048]{2,1,0:T(8,128)} %reduce-scatter.7.cloned.1.call-done) | copy-start | bytes 1179652
  520.3 259.3 %copy-start.56 = (f32[2,24]{1,0:T(2,128)}, f32[2,24]{1,0:T(2,128)S(1)}, u32[]{:S(2)}) copy-start(f32[2,24]{1,0:T(2,128)S(1)} %broadcast_multiply_fusion.4) | copy-start | bytes 580
  (58 other events, 279.7 us)
Sparse Core Ops, SparseCore 0:
  10.9 84.7 all-gather.4
  98.6 68.3 all-gather.6
  169.8 57.5 all-gather.8
  243.1 113.4 reduce-scatter.8
  364.1 154.9 reduce-scatter.6
  525.9 204.0 reduce-scatter.4
where the time goes:
time: 794 us; the launch traced here: 787 us
  waiting for transfers between devices  361 us (45%)
  matrix products  187 us (24%)
  blocking collectives  111 us (14%)
  local copies, waits for them, and re-layouts  64.9 us (8%)
  other arithmetic  46.3 us (6%)
  between operations  16.1 us (2%)
    reduce_scatter x1, waiting for transfers between devices, on_device(): lax.psum_scatter(attention_full_grad, ('wide', 'narrow'), scatter_dimensi...  210 us
    reduce_scatter x1, waiting for transfers between devices, on_device(): lax.psum_scatter(expand_full_grad, ('wide', 'narrow'), scatter_dimension=...  111 us
    all_gather x1, blocking collectives, on_device(): lax.all_gather(norm_gains, ('wide', 'narrow'), axis=1, tiled=True)  70.5 us
    unnamed x1, blocking collectives  40.4 us
    dot_general x11, matrix products, matmul_nt(): lax.dot_general(left, right, (((1,), (1,)), ((), ())), preferred_element_...  40 us
    all_gather x1, waiting for transfers between devices, on_device(): lax.all_gather(contract_weights, ('wide', 'narrow'), axis=0, tiled=True)  37.4 us
    dot_general x11, matrix products, matmul_tn(): lax.dot_general(left, right, (((0,), (0,)), ((), ())), preferred_element_...  33.9 us
    dot_general x11, matrix products, matmul(): return jnp.dot(left, right, preferred_element_type=jnp.float32)  33.3 us
  transfers between devices with their start and end apart: 6, of which 3 were waited for; matrix products, arithmetic and copies ran while one was open for 33% of the time, Pallas kernels for 0%

commit v1 on v0

v1 whole, which is shorter than its diff:
```python
import functools
import math

import jax
import jax.numpy as jnp
import numpy as np
from jax import lax
from jax.experimental import pallas as pl
from jax.experimental.pallas import tpu as pltpu
from jax.sharding import PartitionSpec as P

D = 768
HEADS = 12
FF = 2048
BUCKETS = 32
MAX_DIST = 128
TGT_LEN = 512
MEM_LEN = 512
WIDE = 256
COLS = D // WIDE
BLOCKS = FF // WIDE
PAIRS = HEADS // 2
QROWS = 128

NEG_FILL = -1000000000.0
EPSILON = 1e-06
TINY = 1e-30
STEP_RATE = 0.01
AXES = ("wide", "narrow")
F32 = jnp.float32
BF16 = jnp.bfloat16
MIB = 1024 * 1024
VMEM = pltpu.VMEM


def bucket_onehot(length, bucket_count, far_limit):
    exact_span = bucket_count // 2
    onehot_rows = np.zeros((length, bucket_count), np.float32)
    for distance in range(length):
        if distance < exact_span:
            bucket_id = distance
        else:
            bucket_id = min(
                bucket_count - 1,
                exact_span
                + int(
                    math.log(distance / exact_span)
                    / math.log(far_limit / exact_span)
                    * (bucket_count - exact_span)
                ),
            )
        onehot_rows[distance, bucket_id] = 1.0
    return onehot_rows


def diagonal_onehot():
    t = np.arange(2 * QROWS)
    distance = np.where(t <= QROWS, QROWS - t, 3 * QROWS - t)
    return bucket_onehot(TGT_LEN, BUCKETS, MAX_DIST)[distance]


def mm(left, right):
    return jnp.dot(left, right, preferred_element_type=F32)


def mm_nt(left, right):
    return lax.dot_general(left, right, (((1,), (1,)), ((), ())), preferred_element_type=F32)


def mm_tn(left, right):
    return lax.dot_general(left, right, (((0,), (0,)), ((), ())), preferred_element_type=F32)


def low(values):
    return values.astype(BF16)


def cols(index):
    return slice(index * WIDE, (index + 1) * WIDE)


def inverse_rms(values):
    return lax.rsqrt(jnp.mean(values * values, axis=-1, keepdims=True) + EPSILON)


def norm_back(values, gain, grad):
    scale = inverse_rms(values)
    gain_grad = jnp.sum(values * scale * grad, axis=0, keepdims=True)
    scaled = gain * grad
    inner = jnp.mean(values * scaled, axis=-1, keepdims=True)
    return scale * scaled - values * (scale * scale * scale * inner), gain_grad


def my_index():
    return lax.axis_index("wide") * 2 + lax.axis_index("narrow")


def call(body, outs, in_specs, args, flops, moved, grid=None, scratch=(), limit=48, out_specs=None):
    kwargs = {} if grid is None else {"grid": grid}
    whole = pl.BlockSpec(memory_space=VMEM)
    return pl.pallas_call(
        body,
        out_shape=[jax.ShapeDtypeStruct(*o) for o in outs],
        in_specs=[whole if s is None else s for s in in_specs],
        out_specs=[whole] * len(outs) if out_specs is None else [whole if s is None else s for s in out_specs],
        scratch_shapes=list(scratch),
        compiler_params=pltpu.CompilerParams(vmem_limit_bytes=limit * MIB),
        cost_estimate=pl.CostEstimate(flops=int(flops), bytes_accessed=int(moved), transcendentals=0),
        **kwargs,
    )(*args)


def slot_mask(first, slot):
    high, mid, z = slot >> 3, (slot >> 2) & 1, slot & 3
    dy, dx = (high, mid) if first == 0 else (mid, high)
    return z * 8 + dy * 4 + dx


def put_matrix(ring, acc, own, sib, first, piece, value):
    if not ring:
        own[piece] = value
        return
    acc[...] = value
    me = my_index()
    for out, core in ((own, 0), (sib, 2)):
        for slot in range(16):
            owner = lax.bitwise_xor(me, slot_mask(first, slot) + core)
            rows = acc[pl.ds(pl.multiple_of(owner * 24, 8), 24), :]
            out[slot, piece] = low(rows.reshape(3, 8, WIDE))


def grad_shapes(ring, pieces):
    if ring:
        return [((16, pieces, 3, 8, WIDE), BF16)] * 2
    return [((pieces, D, WIDE), F32)]


def pre_kernel(tok, mem, gains, w, n1, q, k, v, kc, vc):
    x = tok[...].astype(F32)
    normed = low(x * inverse_rms(x) * gains[0:1, :])
    n1[...] = normed
    memory = mem[...]
    for c in range(COLS):
        q[:, cols(c)] = low(mm(normed, w[0, c]))
        k[:, cols(c)] = low(mm(normed, w[1, c]))
        v[:, cols(c)] = low(mm(normed, w[2, c]))
        kc[:, cols(c)] = low(mm(memory, w[5, c]))
        vc[:, cols(c)] = low(mm(memory, w[6, c]))


def halves(block):
    lane = lax.broadcasted_iota(jnp.int32, block.shape, 1)
    zero = jnp.zeros_like(block)
    return jnp.concatenate([jnp.where(lane < 64, block, zero), jnp.where(lane < 64, zero, block)], axis=0)


def side(pair):
    rows = pair.shape[0] // 2
    return jnp.concatenate([pair[:rows], pair[rows:]], axis=1)


def twice(block):
    return jnp.concatenate([block, block], axis=0)


def split_rows(pair, count):
    rows = pair.shape[0] // 2
    return jnp.concatenate([pair[:count], pair[rows : rows + count]], axis=0)


def softmax(scores):
    top = jnp.max(scores, axis=-1, keepdims=True)
    raised = jnp.exp(scores - top)
    return raised * (1.0 / jnp.sum(raised, axis=-1, keepdims=True))


def pair_bias(line):
    rows = [
        pltpu.roll(jnp.broadcast_to(line[h : h + 1, :], (QROWS, 2 * QROWS)), 0, 1, stride=1, stride_axis=0)
        for h in range(2)
    ]
    far = jnp.concatenate([jnp.broadcast_to(line[h : h + 1, 0:1], (QROWS, 1)) for h in range(2)], axis=0)
    return jnp.concatenate(rows, axis=0), far


def self_probs(block, q2, k, bias, far, seg_col, seg_row):
    end = (block + 1) * QROWS
    scores = mm_nt(q2, k[:end])
    if block == 0:
        scores = scores + bias[:, QROWS:]
    elif block == 1:
        scores = scores + bias
    else:
        scores = jnp.concatenate([scores[:, : end - 2 * QROWS] + far, scores[:, end - 2 * QROWS :] + bias], axis=1)
    keep = seg_col == seg_row[:, :end]
    row = lax.broadcasted_iota(jnp.int32, (QROWS, end), 0) + block * QROWS
    keep = keep & (lax.broadcasted_iota(jnp.int32, (QROWS, end), 1) <= row)
    return softmax(jnp.where(twice(keep), scores, NEG_FILL))


def cross_probs(q2, k, seg_col, seg_row):
    keep = seg_col == seg_row
    return softmax(jnp.where(twice(keep), mm_nt(q2, k), NEG_FILL))


def self_forward_kernel(q, k, v, line, seg_col, seg_row, out):
    bias, far = pair_bias(line[0])
    keys, values = k[...], halves(v[...])
    for block in range(TGT_LEN // QROWS):
        rows = slice(block * QROWS, (block + 1) * QROWS)
        probs = self_probs(block, halves(q[rows, :]), keys, bias, far, seg_col[rows, :], seg_row[...])
        out[rows, :] = low(mm(side(low(probs)), split_rows(values, (block + 1) * QROWS)))


def cross_forward_kernel(q, k, v, seg_col, seg_row, out):
    keys, values = k[...], halves(v[...])
    for block in range(TGT_LEN // QROWS):
        rows = slice(block * QROWS, (block + 1) * QROWS)
        probs = cross_probs(halves(q[rows, :]), keys, seg_col[rows, :], seg_row[...])
        out[rows, :] = low(mm(side(low(probs)), values))


def pair_spec(length):
    return pl.BlockSpec((length, 128), lambda p: (0, p))


LINE_SPEC = pl.BlockSpec((1, 2, 2 * QROWS), lambda p: (p, 0, 0))


def mid_kernel(ctx, tok, gains, w, res, n2, qc):
    context = ctx[...]
    for c in range(COLS):
        res[:, cols(c)] = tok[:, cols(c)].astype(F32) + mm(context, w[3, c])
    x = res[...]
    normed = low(x * inverse_rms(x) * gains[1:2, :])
    n2[...] = normed
    for c in range(COLS):
        qc[:, cols(c)] = low(mm(normed, w[4, c]))


def late_kernel(ctx, res1, gains, w, res2, n3):
    context = ctx[...]
    for c in range(COLS):
        res2[:, cols(c)] = res1[:, cols(c)] + mm(context, w[7, c])
    x = res2[...]
    n3[...] = low(x * inverse_rms(x) * gains[2:3, :])


def gelu_pair(gate):
    rate = math.sqrt(2.0 / math.pi)
    square = gate * gate
    bend = jnp.tanh(rate * gate * (1.0 + 0.044715 * square))
    half = 0.5 * (1.0 + bend)
    slope = half + 0.5 * gate * (1.0 - bend * bend) * rate * (1.0 + 3.0 * 0.044715 * square)
    return gate * half, slope


def ffn_kernel(ring, n3, res2, cot, gate_w, lift_w, con_w, out, dn3, *rest):
    grads, (n3t, total, acc, con_acc) = rest[:-4], rest[-4:]
    block = pl.program_id(0)

    @pl.when(block == 0)
    def _():
        n3t[...] = n3[...].T
        total[...] = res2[...]
        dn3[...] = jnp.zeros_like(dn3)

    normed = n3[...]
    gate_rows, lift_rows = gate_w[0, 0], lift_w[0, 0]
    lift = mm(normed, lift_rows)
    active, slope = gelu_pair(mm(normed, gate_rows))
    hidden = low(active * lift)
    back = jnp.zeros(lift.shape, F32)
    for c in range(COLS):
        total[:, cols(c)] += mm(hidden, con_w[c])
        back = back + mm_nt(cot[:, cols(c)], con_w[c])
    gate_grad = low(back * lift * slope)
    lift_grad = low(back * active)
    dn3[...] += mm_nt(gate_grad, gate_rows) + mm_nt(lift_grad, lift_rows)
    turned = hidden.T
    if ring:
        own_a, own_b, sib_a, sib_b = grads
        put_matrix(ring, acc, own_a, sib_a, 0, block, mm(n3t[...], gate_grad))
        put_matrix(ring, acc, own_b, sib_b, 1, block, mm(n3t[...], lift_grad))
        me = my_index()
        near = lax.bitwise_xor(block, lax.shift_right_logical(me, 2))
        dz, dy = lax.shift_right_logical(near, 1), lax.bitwise_and(near, 1)
        inner = lax.bitwise_and(me, 3)
        for c in range(COLS):
            con_acc[...] = mm(turned, cot[:, cols(c)])
            for core in range(2):
                for dx in range(2):
                    place = lax.bitwise_xor(inner, core * 2 + dx)
                    rows = low(con_acc[pl.ds(pl.multiple_of(place * 64, 8), 64), :].reshape(8, 8, WIDE))
                    (own_a, sib_a)[core][dy * 8 + dx * 4 + dz, 8:12, c] = rows[:4]
                    (own_b, sib_b)[core][dx * 8 + dy * 4 + dz, 8:12, c] = rows[4:]
    else:
        gate_out, lift_out, con_out = grads
        gate_out[block] = mm(n3t[...], gate_grad)
        lift_out[block] = mm(n3t[...], lift_grad)
        for c in range(COLS):
            con_out[c, pl.ds(pl.multiple_of(block * WIDE, 8), WIDE), :] = mm(turned, cot[:, cols(c)])

    @pl.when(block == BLOCKS - 1)
    def _():
        out[...] = low(total[...])


def third_back_kernel(dn3, res2, cot, gains, w, r2g, ccg, gg):
    back, gain_grad = norm_back(res2[...], gains[2:3, :], dn3[...])
    gg[...] = gain_grad
    grad = cot[...].astype(F32) + back
    r2g[...] = grad
    cross_low = low(grad)
    total = mm_nt(cross_low[:, cols(0)], w[7, 0])
    for c in range(1, COLS):
        total = total + mm_nt(cross_low[:, cols(c)], w[7, c])
    ccg[...] = low(total)


def backward_block(probs, q2, dc2, keys2, values, dq, dk, dv, rows, end):
    prob_grad = mm_nt(dc2, values[:end])
    moved = probs * prob_grad
    score_grad = low(moved - probs * jnp.sum(moved, axis=-1, keepdims=True))
    dq[rows, :] = low(mm(side(score_grad), split_rows(keys2, end)))
    dk[:end, :] += mm_tn(score_grad, q2)
    dv[:end, :] += mm_tn(low(probs), dc2)
    return score_grad


def cross_back_kernel(q, k, v, dc, seg_col, seg_row, dq, dk, dv, dk_acc, dv_acc):
    dk_acc[...] = jnp.zeros_like(dk_acc)
    dv_acc[...] = jnp.zeros_like(dv_acc)
    keys, values = k[...], v[...]
    keys2 = halves(keys)
    for block in range(TGT_LEN // QROWS):
        rows = slice(block * QROWS, (block + 1) * QROWS)
        q2 = halves(q[rows, :])
        probs = cross_probs(q2, keys, seg_col[rows, :], seg_row[...])
        backward_block(probs, q2, halves(dc[rows, :]), keys2, values, dq, dk_acc, dv_acc, rows, MEM_LEN)
    dk[...] = low(dk_acc[...])
    dv[...] = low(dv_acc[...])


def diagonal_sums(grid, start):
    width = 2 * QROWS
    group = grid[start : start + 8, :]
    for shift in range(8, QROWS, 8):
        group = group + pltpu.roll(grid[start + shift : start + shift + 8, :], width - shift, 1)
    row = lax.broadcasted_iota(jnp.int32, group.shape, 0)
    for bit in (1, 2, 4):
        group = jnp.where((row & bit) != 0, pltpu.roll(group, width - bit, 1), group)
    return jnp.sum(group, axis=0, keepdims=True)


def self_back_kernel(q, k, v, dc, line, seg_col, seg_row, dq, dk, dv, diag, dk_acc, dv_acc, near):
    dk_acc[...] = jnp.zeros_like(dk_acc)
    dv_acc[...] = jnp.zeros_like(dv_acc)
    bias, far = pair_bias(line[0])
    keys, values = k[...], v[...]
    keys2 = halves(keys)
    far_sum = jnp.zeros((2 * QROWS, QROWS), F32)
    for block in range(TGT_LEN // QROWS):
        rows = slice(block * QROWS, (block + 1) * QROWS)
        end = (block + 1) * QROWS
        q2 = halves(q[rows, :])
        probs = self_probs(block, q2, keys, bias, far, seg_col[rows, :], seg_row[...])
        score_grad = backward_block(
            probs, q2, halves(dc[rows, :]), keys2, values, dq, dk_acc, dv_acc, rows, end
        ).astype(F32)
        if block == 0:
            near[:, :QROWS] = jnp.zeros((2 * QROWS, QROWS), F32)
            near[:, QROWS:] = score_grad
        else:
            near[...] += score_grad[:, end - 2 * QROWS :]
        for other in range(block - 1):
            far_sum = far_sum + score_grad[:, other * QROWS : (other + 1) * QROWS]
    dk[...] = low(dk_acc[...])
    dv[...] = low(dv_acc[...])
    lane = lax.broadcasted_iota(jnp.int32, (1, 2 * QROWS), 1)
    for h in range(2):
        beyond = jnp.sum(far_sum[h * QROWS : (h + 1) * QROWS, :], keepdims=True)
        diag[0, h : h + 1, :] = diagonal_sums(near, h * QROWS) + jnp.where(lane == 0, beyond, 0.0)


def second_back_kernel(ring, dq, dk, dv, mem, res1, r2g, gains, w, ctxs, ctxc, n2, mg, r1g, csg, gg, *rest):
    grads, acc = rest[:-1], rest[-1]
    query_grad, key_grad, value_grad = dq[...], dk[...], dv[...]
    back = mm_nt(query_grad[:, cols(0)], w[4, 0])
    for c in range(1, COLS):
        back = back + mm_nt(query_grad[:, cols(c)], w[4, c])
    moved, gain_grad = norm_back(res1[...], gains[1:2, :], back)
    gg[...] = gain_grad
    grad = r2g[...] + moved
    r1g[...] = grad
    self_low, cross_low = low(grad), low(r2g[...])
    total = mm_nt(self_low[:, cols(0)], w[3, 0])
    for c in range(1, COLS):
        total = total + mm_nt(self_low[:, cols(c)], w[3, c])
    csg[...] = low(total)
    total = mm_nt(key_grad[:, cols(0)], w[5, 0]) + mm_nt(value_grad[:, cols(0)], w[6, 0])
    for c in range(1, COLS):
        total = total + mm_nt(key_grad[:, cols(c)], w[5, c]) + mm_nt(value_grad[:, cols(c)], w[6, c])
    mg[...] = low(total)
    memory_t = mem[...].T
    for matrix, left, right in (
        (3, ctxs[...].T, self_low),
        (4, n2[...].T, query_grad),
        (5, memory_t, key_grad),
        (6, memory_t, value_grad),
        (7, ctxc[...].T, cross_low),
    ):
        for c in range(COLS):
            put_piece(ring, grads, acc, (matrix - 3) * COLS + c, 8, mm(left, right[:, cols(c)]))


def put_piece(ring, grads, acc, index, split, value):
    if not ring:
        grads[0][index] = value
        return
    own_a, own_b, sib_a, sib_b = grads
    if index < split:
        put_matrix(ring, acc, own_a, sib_a, 0, index, value)
    else:
        put_matrix(ring, acc, own_b, sib_b, 1, index - split, value)


def first_grads_kernel(ring, dq, dk, dv, n1, *rest):
    grads, acc = rest[:-1], rest[-1]
    left = n1[...].T
    for matrix, right in enumerate((dq, dk, dv)):
        for c in range(COLS):
            put_piece(ring, grads, acc, matrix * COLS + c, 5, mm(left, right[:, cols(c)]))


def first_back_kernel(dq, dk, dv, tok, r1g, gains, w, ig, gg):
    back = None
    for matrix, right in enumerate((dq, dk, dv)):
        for c in range(COLS):
            term = mm_nt(right[:, cols(c)], w[matrix, c])
            back = term if back is None else back + term
    moved, gain_grad = norm_back(tok[...].astype(F32), gains[0:1, :], back)
    gg[...] = gain_grad
    ig[...] = low(r1g[...] + moved)


def hop(values, mask):
    return lax.ppermute(values, AXES, [(k, k ^ mask) for k in range(32)])


def after(values, *earlier):
    return lax.optimization_barrier((values,) + earlier)[0]


def place_kernel(plan, targets, count, *refs):
    ins, outs, sem = refs[:count], refs[count:-1], refs[-1]
    me = my_index()
    copies = []
    for ref, (masks, low_piece, high_piece) in zip(ins, plan):
        for index, mask in enumerate(masks):
            owner = lax.bitwise_xor(me, mask)
            for out, first, last, start, column in targets:
                begin, end = max(low_piece, first), min(high_piece, last)
                if begin >= end:
                    continue
                pieces = pl.ds(begin - low_piece, end - begin)
                into = pl.ds(start + begin - first, end - begin)
                if column is None:
                    pair = (ref.at[index, pieces], outs[out].at[into, owner])
                else:
                    pair = (ref.at[index, pieces, column], outs[out].at[column, owner, into])
                copies.append(pltpu.make_async_copy(*pair, sem.at[len(copies)]))
                copies[-1].start()
    for copy in copies:
        copy.wait()


def place(arrays, outs, targets):
    plan = [a[1:] for a in arrays]
    return call(
        functools.partial(place_kernel, plan, targets, len(arrays)),
        [(o, BF16) for o in outs],
        [pl.BlockSpec(memory_space=pl.ANY)] * len(arrays),
        [a[0] for a in arrays],
        0,
        2 * 2 * math.prod(outs[0]),
        scratch=[pltpu.SemaphoreType.DMA((320,))],
        limit=32,
    )


def spread_start(chunks, *earlier):
    own = jnp.stack(chunks) if len(chunks) > 1 else chunks[0][None]
    if earlier:
        own = after(own, *earlier)
    return own, hop(own, 1), hop(own, 4)


def spread_end(started, masks, half):
    own, by_x, by_y = started
    pieces = own.shape[1]
    first = hop(by_x[:, :half], 4)
    second = hop(by_y[:, half:], 1)
    shift = lambda d: [m + d for m in masks]
    return [
        (own, shift(0), 0, pieces),
        (by_x, shift(1), 0, pieces),
        (by_y, shift(4), 0, pieces),
        (first, shift(5), 0, half),
        (second, shift(5), half, pieces),
    ]


def with_core(arrays):
    return arrays + [(hop(a, 2), [m + 2 for m in masks], lo, hi) for a, masks, lo, hi in arrays]


def gather_ring(attention, expand, contract, gains):
    attention_pieces = attention.reshape(8, 24, COLS, WIDE).transpose(0, 2, 1, 3).reshape(24, 3, 8, WIDE)
    gain_piece = jnp.pad(gains.reshape(1, 3, 1, 24), ((0, 0), (0, 0), (0, 7), (0, WIDE - 24)))
    first = jnp.concatenate([attention_pieces, gain_piece])
    expand_pieces = expand.reshape(2, 24, BLOCKS, WIDE).transpose(0, 2, 1, 3).reshape(2, BLOCKS, 3, 8, WIDE)
    contract_pieces = contract.reshape(8, 8, COLS, WIDE).transpose(0, 2, 1, 3)
    second = jnp.concatenate([expand_pieces[0], contract_pieces[:4], expand_pieces[1], contract_pieces[4:]])
    half_first, half_second = 13, 12

    z1 = hop(first, 8)
    z3 = hop(after(first, z1), 24)
    s0 = spread_start([first, z1])
    z2 = hop(after(z3, s0[1], s0[2]), 8)
    a0 = spread_end(s0, [0, 8], half_first)
    s1 = spread_start([z2, z3], s0[1], s0[2])
    v1 = hop(after(second, z2), 8)
    v3 = hop(after(second, v1), 24)
    v2 = hop(v3, 8)
    a1 = spread_end(s1, [16, 24], half_first)
    t0 = spread_start([second, v1], s1[1], s1[2], a0[3][0], a0[4][0])
    b0 = spread_end(t0, [0, 8], half_second)
    t1 = spread_start([v2, v3], t0[1], t0[2], a1[3][0], a1[4][0])
    b1 = spread_end(t1, [16, 24], half_second)
    square, gains_out = place(
        with_core(a0) + with_core(a1),
        [(24, 32, 3, 8, WIDE), (1, 32, 3, 8, WIDE)],
        [(0, 0, 24, 0, None), (1, 24, 25, 0, None)],
    )
    wide, narrow = place(
        with_core(b0) + with_core(b1),
        [(16, 32, 3, 8, WIDE), (COLS, 32, 8, 8, WIDE)],
        [(0, 0, 8, 0, None), (0, 12, 20, 8, None)]
        + [(1, 8, 12, 0, c) for c in range(COLS)]
        + [(1, 20, 24, 4, c) for c in range(COLS)],
    )
    gain_rows = gains_out[0, :, :, 0, :24].transpose(1, 0, 2).reshape(3, D)
    return (
        square.reshape(8, COLS, D, WIDE),
        wide.reshape(2, BLOCKS, D, WIDE),
        narrow.reshape(COLS, FF, WIDE),
        gain_rows,
    )


def gather_plain(attention, expand, contract, gains):
    attention, expand, contract, gains = (
        lax.all_gather(attention, AXES, axis=1, tiled=True),
        lax.all_gather(expand, AXES, axis=1, tiled=True),
        lax.all_gather(contract, AXES, axis=0, tiled=True),
        lax.all_gather(gains, AXES, axis=1, tiled=True),
    )
    return (
        attention.reshape(8, D, COLS, WIDE).transpose(0, 2, 1, 3),
        expand.reshape(2, D, BLOCKS, WIDE).transpose(0, 2, 1, 3),
        contract.reshape(FF, COLS, WIDE).transpose(1, 0, 2),
        gains,
    )


def total(*terms):
    result = terms[0].astype(F32)
    for term in terms[1:]:
        result = result + term.astype(F32)
    return result


def scatter_ring(grads, *earlier):
    own_a, own_b, sib_a, sib_b = grads
    from_a, from_b = hop(sib_a, 2), hop(sib_b, 2)
    send_a = low(total(own_a[8:], from_a[8:]))
    send_b = low(total(own_b[8:], from_b[8:]))
    a1, b1 = hop(send_a, 4), hop(send_b, 1)
    next_a = low(total(own_a[4:8], from_a[4:8], a1[4:]))
    next_b = low(total(own_b[4:8], from_b[4:8], b1[4:]))
    a2, b2 = hop(next_a, 1), hop(next_b, 4)
    mine_a = total(own_a[:4], from_a[:4], a1[:4], a2)
    mine_b = total(own_b[:4], from_b[:4], b1[:4], b2)
    mine = jnp.concatenate([mine_a, mine_b], axis=1)
    near = hop(low(mine[1:3]), 8)
    far = hop(low(mine[3] + near[1].astype(F32)), 24)
    return total(mine[0], near[0], far)


def scatter_plain(pieces, shape, axis):
    count = pieces.shape[0]
    if axis == 0:
        whole = pieces.transpose(1, 0, 2).reshape(shape)
    else:
        per = shape[2] // WIDE
        whole = pieces.reshape(shape[0], per, shape[1], WIDE).transpose(0, 2, 1, 3).reshape(shape)
    return lax.psum_scatter(whole, AXES, scatter_dimension=axis, tiled=True)


def sum_ring(values):
    values = values + hop(values, 2)
    values = (values + hop(values, 1)) + (hop(values, 4) + hop(values, 5))
    return (values + hop(values, 8)) + (hop(values, 16) + hop(values, 24))


def factored_stats(grad_shard, total_rows):
    squares = grad_shard * grad_shard + TINY
    return (jnp.mean(squares, axis=-1), jnp.sum(squares, axis=-2) / total_rows)


def factored_update(weight_shard, grad_shard, row_stat, column_stat):
    scale = jnp.mean(column_stat, axis=-1, keepdims=True)[..., None]
    second = row_stat[..., :, None] * column_stat[..., None, :] / scale
    return weight_shard.astype(F32) - STEP_RATE * grad_shard * lax.rsqrt(second)


def without_outputs(stats):
    return jnp.concatenate([stats[0:3], stats[4:7]], axis=0)


def output_pair(stats):
    return jnp.stack([stats[3], stats[7]])


def on_device(
    ring,
    tokens,
    memory,
    target_segments,
    memory_segments,
    attention_weights,
    expand_weights,
    contract_weights,
    norm_gains,
    bucket_table,
    cotangent,
):
    rows = tokens.shape[0]
    gather = gather_ring if ring else gather_plain
    square, wide, narrow, gains = gather(attention_weights, expand_weights, contract_weights, norm_gains)
    gains = gains.astype(F32)
    spread_buckets = jnp.asarray(diagonal_onehot())
    lines = jnp.dot(
        bucket_table.T.astype(F32), spread_buckets.T, precision=lax.Precision.HIGHEST, preferred_element_type=F32
    ).reshape(PAIRS, 2, 2 * QROWS)
    target_col, target_row = target_segments.reshape(rows, 1), target_segments.reshape(1, rows)
    memory_row = memory_segments.reshape(1, rows)
    act, act32 = ((rows, D), BF16), ((rows, D), F32)
    size = rows * D
    product = 2 * size * D
    none = [None]

    n1, q, k, v, kc, vc = call(
        pre_kernel, [act] * 6, none * 4, (tokens, memory, gains, square), 5 * product, 2 * (8 * size + 5 * D * D)
    )
    pair = pair_spec(rows)
    heads_work = 2 * HEADS * rows * rows * 256
    ctxs = call(
        self_forward_kernel,
        [act],
        [pair] * 3 + [LINE_SPEC, None, None],
        (q, k, v, lines, target_col, target_row),
        2 * heads_work,
        8 * size,
        grid=(PAIRS,),
        out_specs=[pair],
    )[0]
    res1, n2, qc = call(
        mid_kernel, [act32, act, act], none * 4, (ctxs, tokens, gains, square), 2 * product, 14 * size + 4 * D * D
    )
    ctxc = call(
        cross_forward_kernel,
        [act],
        [pair] * 3 + [None, None],
        (qc, kc, vc, target_col, memory_row),
        2 * heads_work,
        8 * size,
        grid=(PAIRS,),
        out_specs=[pair],
    )[0]
    res2, n3 = call(late_kernel, [act32, act], none * 4, (ctxc, res1, gains, square), product, 14 * size)

    expand_block = lambda m: pl.BlockSpec((1, 1, D, WIDE), lambda b: (m, b, 0, 0))
    if ring:
        grad_outs = [((16, 12, 3, 8, WIDE), BF16)] * 4
    else:
        grad_outs = [((BLOCKS, D, WIDE), F32)] * 2 + [((COLS, FF, WIDE), F32)]
    output, dn3, *ffn_grads = call(
        functools.partial(ffn_kernel, ring),
        [act, act32] + grad_outs,
        none * 3 + [expand_block(0), expand_block(1), pl.BlockSpec((COLS, WIDE, WIDE), lambda b: (0, b, 0))],
        (n3, res2, cotangent, wide, wide, narrow),
        9 * 2 * rows * D * FF,
        4 * 3 * D * FF,
        grid=(BLOCKS,),
        scratch=[
            VMEM((D, rows), BF16),
            VMEM((rows, D), F32),
            VMEM((D, WIDE), F32),
            VMEM((WIDE, WIDE), F32),
        ],
    )

    r2g, ccg, gain_three = call(
        third_back_kernel,
        [act32, act, ((1, D), F32)],
        none * 5,
        (dn3, res2, cotangent, gains, square),
        product,
        16 * size,
    )
    acc = VMEM((D, WIDE), F32)
    head_acc = VMEM((rows, 128), F32)
    dqc, dkc, dvc = call(
        cross_back_kernel,
        [act] * 3,
        [pair] * 4 + [None, None],
        (qc, kc, vc, ccg, target_col, memory_row),
        5 * heads_work,
        14 * size,
        grid=(PAIRS,),
        scratch=[head_acc, head_acc],
        out_specs=[pair] * 3,
    )
    second_grads = grad_shapes(ring, 8) + grad_shapes(ring, 7) if ring else grad_shapes(ring, 15)
    if ring:
        second_grads = [second_grads[0], second_grads[2], second_grads[1], second_grads[3]]
    memory_grad, r1g, csg, gain_two, *cross_grads = call(
        functools.partial(second_back_kernel, ring),
        [act, act32, act, ((1, D), F32)] + second_grads,
        none * 11,
        (dqc, dkc, dvc, memory, res1, r2g, gains, square, ctxs, ctxc, n2),
        9 * product,
        24 * size + 20 * D * D,
        scratch=[acc],
    )
    dqs, dks, dvs, diag = call(
        self_back_kernel,
        [act] * 3 + [((PAIRS, 2, 2 * QROWS), F32)],
        [pair] * 4 + [LINE_SPEC, None, None],
        (q, k, v, csg, lines, target_col, target_row),
        5 * heads_work,
        14 * size,
        grid=(PAIRS,),
        scratch=[head_acc, head_acc, VMEM((2 * QROWS, 2 * QROWS), F32)],
        out_specs=[pair] * 3 + [LINE_SPEC],
    )
    first_grads = grad_shapes(ring, 5) + grad_shapes(ring, 4) if ring else grad_shapes(ring, 9)
    if ring:
        first_grads = [first_grads[0], first_grads[2], first_grads[1], first_grads[3]]
    self_grads = call(
        functools.partial(first_grads_kernel, ring),
        first_grads,
        none * 4,
        (dqs, dks, dvs, n1),
        3 * product,
        8 * size + 6 * D * D,
        scratch=[acc],
    )
    input_grad, gain_one = call(
        first_back_kernel,
        [act, ((1, D), F32)],
        none * 7,
        (dqs, dks, dvs, tokens, r1g, gains, square),
        3 * product,
        16 * size + 6 * D * D,
    )
    bucket_part = jnp.dot(
        spread_buckets.T, diag.reshape(HEADS, 2 * QROWS).T, precision=lax.Precision.HIGHEST, preferred_element_type=F32
    )
    gains_part = jnp.concatenate([gain_one, gain_two, gain_three])

    if ring:
        ffn_share = scatter_ring(ffn_grads)
        cross_share = scatter_ring(cross_grads)
        self_share = scatter_ring(self_grads)
        squares = jnp.concatenate([self_share, cross_share]).reshape(8, COLS, 24, WIDE)
        attention_grad = squares.transpose(0, 2, 1, 3).reshape(8, 24, D)
        expand_grad = jnp.stack([ffn_share[0:8], ffn_share[12:20]])
        expand_grad = expand_grad.reshape(2, BLOCKS, 24, WIDE).transpose(0, 2, 1, 3).reshape(2, 24, FF)
        contract_grad = jnp.concatenate([ffn_share[8:12], ffn_share[20:24]])
        contract_grad = contract_grad.transpose(0, 2, 1, 3).reshape(64, D)
    else:
        pieces = jnp.concatenate([self_grads[0], cross_grads[0]])
        attention_grad = scatter_plain(pieces, (8, D, D), 1)
        expand_grad = scatter_plain(jnp.stack(ffn_grads[:2]), (2, D, FF), 1)
        contract_grad = scatter_plain(ffn_grads[2], (FF, D), 0)

    attention_rows, attention_part = factored_stats(attention_grad, D)
    expand_rows, expand_part = factored_stats(expand_grad, D)
    contract_rows, contract_part = factored_stats(contract_grad, FF)
    parts = (attention_part, expand_part, contract_part, bucket_part, gains_part)
    if ring:
        flat = jnp.concatenate([p.reshape(-1) for p in parts]).reshape(-1, 128)
        flat = sum_ring(flat).reshape(-1)
        sums, start = [], 0
        for p in parts:
            sums.append(flat[start : start + p.size].reshape(p.shape))
            start += p.size
    else:
        sums = lax.psum(parts, AXES)
    attention_columns, expand_columns, contract_columns, bucket_grad, gains_sum = sums
    attention_new = factored_update(attention_weights, attention_grad, attention_rows, attention_columns)
    expand_new = factored_update(expand_weights, expand_grad, expand_rows, expand_columns)
    contract_new = factored_update(contract_weights, contract_grad, contract_rows, contract_columns)
    share_width = attention_rows.shape[1]
    share_start = lax.axis_index(AXES) * share_width
    column_share = lax.dynamic_slice_in_dim(attention_columns, share_start, share_width, 1)
    gains_grad = lax.dynamic_slice_in_dim(gains_sum, share_start, share_width, 1)
    projection_statistics = jnp.stack([output_pair(attention_rows), output_pair(column_share)])
    return (
        output,
        input_grad,
        memory_grad,
        attention_grad,
        expand_grad,
        contract_grad,
        gains_grad,
        bucket_grad,
        without_outputs(attention_rows),
        without_outputs(attention_columns),
        expand_rows,
        expand_columns,
        contract_rows,
        contract_columns,
        attention_new,
        expand_new,
        contract_new,
        projection_statistics,
    )


def solution(mesh):
    ring = dict(mesh.shape) == {"wide": 16, "narrow": 2}
    rows, both = P(AXES, None), P(None, AXES, None)
    placed = (rows, rows, P(AXES), P(AXES), both, both, rows, P(None, AXES), P(), rows)
    return jax.shard_map(
        functools.partial(on_device, ring),
        mesh=mesh,
        in_specs=placed,
        out_specs=(
            rows,
            rows,
            rows,
            both,
            both,
            rows,
            P(None, AXES),
            P(),
            P(None, AXES),
            P(),
            P(None, AXES),
            P(),
            P(AXES),
            P(),
            both,
            both,
            rows,
            P(None, None, AXES),
        ),
        check_vma=False,
    )
```

time: 794 us -> 455 us (0.57)
  waiting for transfers between devices: 361 us -> 149 us
  matrix products: 187 us -> 0.49 us
  Pallas kernels: 0 us -> 146 us
  blocking collectives: 111 us -> 0 us
  starting transfers between devices: 0.64 us -> 72.8 us
  local copies, waits for them, and re-layouts: 64.9 us -> 47.8 us
  other arithmetic: 46.3 us -> 31.8 us
  between operations: 16.1 us -> 2.85 us
    reduce_scatter x3 -> x0, waiting for transfers between devices: 321 us -> none  [the longest x1 210 us: on_device(): lax.psum_scatter(attention_full_grad, ('wide', 'narrow'), scatter_dimensi...]
    dot_general x47 -> x2, matrix products: 187 us -> 0.49 us  [the longest x1 0.33 us: on_device(): jnp.dot(spread_buckets.T, diag.reshape(HEADS, 2 * QROWS).T, precision=lax...]
    ppermute x0 -> x73, waiting for transfers between devices: none -> 149 us  [hop(): return lax.ppermute(values, AXES, [(k, k ^ mask) for k in range(32)])]
    pallas_call x0 -> x14, Pallas kernels: none -> 146 us  [call(): pl.pallas_call(body, out_shape=[jax.ShapeDtypeStruct(*o) for o in outs],...]
    ppermute x0 -> x73, starting transfers between devices: none -> 72.8 us  [hop(): return lax.ppermute(values, AXES, [(k, k ^ mask) for k in range(32)])]
    all_gather x1 -> x0, blocking collectives: 70.5 us -> none  [on_device(): lax.all_gather(norm_gains, ('wide', 'narrow'), axis=1, tiled=True)]
    unnamed x1 -> x0, blocking collectives: 40.4 us -> none
    all_gather x3 -> x0, waiting for transfers between devices: 37.4 us -> none  [the longest x1 37.4 us: on_device(): lax.all_gather(contract_weights, ('wide', 'narrow'), axis=0, tiled=True)]
  transfers between devices with their start and end apart: 6 -> 73, of which waited for: 3 -> 30; matrix products, arithmetic and copies ran while one was open for 33% -> 7% of each run, Pallas kernels for 0% -> 12%
where the time goes in v1:
time: 455 us; the launch traced here: 450 us
  waiting for transfers between devices  149 us (33%)
  Pallas kernels  146 us (32%)
  starting transfers between devices  72.8 us (16%)
  local copies, waits for them, and re-layouts  47.8 us (11%)
  other arithmetic  31.8 us (7%)
    ppermute x73, waiting for transfers between devices, hop(): return lax.ppermute(values, AXES, [(k, k ^ mask) for k in range(32)])  149 us
    pallas_call x14, Pallas kernels, call(): pl.pallas_call(body, out_shape=[jax.ShapeDtypeStruct(*o) for o in outs],...  146 us
    ppermute x73, starting transfers between devices, hop(): return lax.ppermute(values, AXES, [(k, k ^ mask) for k in range(32)])  72.8 us
    unnamed x202, local copies, waits for them, and re-layouts  39.3 us
    convert_element_type x15, other arithmetic, low(): return values.astype(BF16)  16.3 us
  transfers between devices with their start and end apart: 73, of which 30 were waited for; matrix products, arithmetic and copies ran while one was open for 7% of the time, Pallas kernels for 12%

profile of v1, /device:TPU:0, one launch (start us, length us, event | category | flops | bytes accessed | tf_op | source)
XLA Modules:
  0.0 450.1 jit_solution(5675672084681306419)
XLA Ops:
  5.0 7.3 %collective-permute-done = bf16[25,3,8,256]{3,2,1,0:T(8,128)(2,1)S(1)} collective-permute-done((bf16[25,3,8,256]{3,2,1,0:T(8,128)(2,1)S(1)}, bf16[25,3,8,256]{3,2,1,0:T(8,128)(2,1)S(1)}, u32[]{:S(2)}, u32[]{:S(2)}) %collective-permute-start) | collective-permute-done | bytes 307232 | tf_op jit(solution)/shard_map/ppermute | solution.py:448
  19.2 5.9 %collective-permute-done.10 = bf16[25,3,8,256]{3,2,1,0:T(8,128)(2,1)S(1)} collective-permute-done((bf16[25,3,8,256]{3,2,1,0:T(8,128)(2,1)S(1)}, bf16[25,3,8,256]{3,2,1,0:T(8,128)(2,1)S(1)}, u32[]{:S(2)}, u32[]{:S(2)}) %collective-permute-start.10) | collective-permute-done | bytes 307232 | tf_op jit(solution)/shard_map/ppermute | solution.py:448
  45.9 6.9 %collective-permute-done.12.refs_11_ = bf16[2,25,3,8,256]{4,3,2,1,0:T(8,128)(2,1)S(1)} collective-permute-done((bf16[2,25,3,8,256]{4,3,2,1,0:T(8,128)(2,1)S(1)}, bf16[2,25,3,8,256]{4,3,2,1,0:T(8,128)(2,1)S(1)}, u32[]{:S(2)}, u32[]{:S(2)}) %collective-permute-start.12) | collective-permute-done | bytes 614432 | tf_op jit(solution)/shard_map/ppermute | solution.py:448
  55.2 6.4 %collective-permute-done.31 = bf16[24,3,8,256]{3,2,1,0:T(8,128)(2,1)S(1)} collective-permute-done((bf16[24,3,8,256]{3,2,1,0:T(8,128)(2,1)S(1)}, bf16[24,3,8,256]{3,2,1,0:T(8,128)(2,1)S(1)}, u32[]{:S(2)}, u32[]{:S(2)}) %collective-permute-start.31) | collective-permute-done | bytes 294944 | tf_op jit(solution)/shard_map/ppermute | solution.py:448
  78.1 8.8 %collective-permute-done.23.refs_2_ = bf16[2,24,3,8,256]{4,3,2,1,0:T(8,128)(2,1)S(1)} collective-permute-done((bf16[2,24,3,8,256]{4,3,2,1,0:T(8,128)(2,1)S(1)}, bf16[2,24,3,8,256]{4,3,2,1,0:T(8,128)(2,1)S(1)}, u32[]{:S(2)}, u32[]{:S(2)}) %collective-permute-start.23) | collective-permute-done | bytes 589856 | tf_op jit(solution)/shard_map/ppermute | solution.py:448
  98.2 13.5 %collective-permute-done.24.refs_3_ = bf16[2,12,3,8,256]{4,3,2,1,0:T(8,128)(2,1)} collective-permute-done((bf16[2,12,3,8,256]{4,3,2,1,0:T(8,128)(2,1)S(1)}, bf16[2,12,3,8,256]{4,3,2,1,0:T(8,128)(2,1)}, u32[]{:S(2)}, u32[]{:S(2)}) %collective-permute-start.24) | collective-permute-done | bytes 294944 | tf_op jit(solution)/shard_map/ppermute | solution.py:448
  139.8 7.3 %shard_map.251 = (bf16[512,768]{1,0:T(8,128)(2,1)S(1)}, bf16[512,768]{1,0:T(8,128)(2,1)S(1)}, bf16[512,768]{1,0:T(8,128)(2,1)S(1)}, bf16[512,768]{1,0:T(8,128)(2...) custom-call(bf16[512,768]{1,0:T(8,128)(2,1)S(1)} %copy-done.3, bf16[512,768]{1,0:T(8,128)(2,1)} %mem.3, ...), custom_call_target="tpu_custom_call" | custom-call | flops 3019898880 | bytes 12189696 | tf_op jit(solution)/shard_map/pallas_call | solution.py:101
  152.0 10.9 %shard_map.252.ctx.ctxs = bf16[512,768]{1,0:T(8,128)(2,1)S(1)} custom-call(bf16[512,768]{1,0:T(8,128)(2,1)S(1)} %get-tuple-element.75.q, bf16[512,768]{1,0:T(8,128)(2,1)S(1)} %get-tuple-element.76.k, bf16[512,768]{1,0:T(8,128)(2,1)S(1)} %get-tuple-element.77.v, f32[6,2,256]{2,1,0:T(2,128)S(1)} %reshape.204.line, s32[512,1]{1,0:T(8,128)S(1)} %copy-done.52, ...), custom_call_target="tpu_custom_call" | custom-call | flops 3221225472 | bytes 3145728 | tf_op jit(solution)/shard_map/pallas_call | solution.py:101
  163.8 5.6 %shard_map.253 = (f32[512,768]{1,0:T(8,128)S(1)}, bf16[512,768]{1,0:T(8,128)(2,1)S(1)}, bf16[512,768]{1,0:T(8,128)(2,1)S(1)}) custom-call(bf16[512,768]{1,0:T(8,128)(2,1)S(1)} %shard_map.252.ctx.ctxs, bf16[512,768]{1,0:T(8,128)(2,1)S(1)} %copy-done.3, f32[3,768]{1,0:T(4,128)S(1)} %reshape.223.gains, bf16[8,3,768,256]{3,2,1,0:T(8,128)(2,1)} %bitcast.109), custom_call_target="tpu_custom_call" | custom-call | flops 1207959552 | bytes 7864320 | tf_op jit(solution)/shard_map/pallas_call | solution.py:101
  170.9 11.7 %shard_map.254.ctx.ctxc = bf16[512,768]{1,0:T(8,128)(2,1)S(1)} custom-call(bf16[512,768]{1,0:T(8,128)(2,1)S(1)} %get-tuple-element.78.q, bf16[512,768]{1,0:T(8,128)(2,1)S(1)} %get-tuple-element.79.k, bf16[512,768]{1,0:T(8,128)(2,1)S(1)} %get-tuple-element.80.v, s32[512,1]{1,0:T(8,128)S(1)} %copy-done.52, s32[1,512]{1,0:T(1,128)S(1)} %bitcast.120), custom_call_target="tpu_custom_call" | custom-call | flops 3221225472 | bytes 3145728 | tf_op jit(solution)/shard_map/pallas_call | solution.py:101
  187.4 6.2 %shard_map.256 = (bf16[16,32,3,8,256]{4,3,2,1,0:T(8,128)(2,1)S(1)}, bf16[3,32,8,8,256]{4,3,2,1,0:T(8,128)(2,1)S(1)}) custom-call(bf16[2,24,3,8,256]{4,3,2,1,0:T(8,128)(2,1)S(1)} %pad_maximum_fusion.3.refs_0_, bf16[2,24,3,8,256]{4,3,2,1,0:T(8,128)(2,1)} %collective-permute-done.22.refs_1_, bf16[2,24,3,8,256]{4,3,2,1,0:T(8,128)(2,1)S(1)} %copy-done.16, ...), custom_call_target="tpu_custom_call" | custom-call | bytes 12582912 | tf_op jit(solution)/shard_map/pallas_call | solution.py:101
  197.8 26.6 %shard_map.257 = (bf16[512,768]{1,0:T(8,128)(2,1)}, f32[512,768]{1,0:T(8,128)S(1)}, bf16[16,12,3,8,256]{4,3,2,1,0:T(8,128)(2,1)}, bf16[16,12,3,8,256]{4,3,2,1,0:...) custom-call(bf16[512,768]{1,0:T(8,128)(2,1)S(1)} %get-tuple-element.82.n3, ...), custom_call_target="tpu_custom_call" | custom-call | flops 14495514624 | bytes 18874368 | tf_op jit(solution)/shard_map/pallas_call | solution.py:101
  224.4 5.6 %shard_map.258 = (f32[512,768]{1,0:T(8,128)S(1)}, bf16[512,768]{1,0:T(8,128)(2,1)S(1)}, f32[1,768]{1,0:T(1,128)S(1)}) custom-call(f32[512,768]{1,0:T(8,128)S(1)} %get-tuple-element.91.dn3, f32[512,768]{1,0:T(8,128)} %copy-done.6, bf16[512,768]{1,0:T(8,128)(2,1)S(1)} %copy-done.25, f32[3,768]{1,0:T(4,128)S(1)} %reshape.223.gains, ...), custom_call_target="tpu_custom_call" | custom-call | flops 603979776 | bytes 6291456 | tf_op jit(solution)/shard_map/pallas_call | solution.py:101
  230.0 18.8 %shard_map.259 = (bf16[512,768]{1,0:T(8,128)(2,1)S(1)}, bf16[512,768]{1,0:T(8,128)(2,1)S(1)}, bf16[512,768]{1,0:T(8,128)(2,1)S(1)}) custom-call(bf16[512,768]{1,0:T(8,128)(2,1)S(1)} %copy-done.60, bf16[512,768]{1,0:T(8,128)(2,1)S(1)} %copy-done.71, bf16[512,768]{1,0:T(8,128)(2,1)S(1)} %copy-done.73, bf16[512,768]{1,0:T(8,128)(2,1)S(1)} %get-tuple-element.92.dc, ...), custom_call_target="tpu_custom_call" | custom-call | flops 8053063680 | bytes 5505024 | tf_op jit(solution)/shard_map/pallas_call | solution.py:101
  248.9 15.6 %shard_map.260 = (bf16[512,768]{1,0:T(8,128)(2,1)}, f32[512,768]{1,0:T(8,128)}, bf16[512,768]{1,0:T(8,128)(2,1)S(1)}, f32[1,768]{1,0:T(1,128)S(1)}, bf16[16,8,3,...) custom-call(bf16[512,768]{1,0:T(8,128)(2,1)S(1)} %get-tuple-element., ...), custom_call_target="tpu_custom_call" | custom-call | flops 5435817984 | bytes 21233664 | tf_op jit(solution)/shard_map/pallas_call | solution.py:101
  264.6 17.6 %shard_map.261 = (bf16[512,768]{1,0:T(8,128)(2,1)S(1)}, bf16[512,768]{1,0:T(8,128)(2,1)S(1)}, bf16[512,768]{1,0:T(8,128)(2,1)S(1)}, f32[6,2,256]{2,1,0:T(2,128)S(1)}) custom-call(bf16[512,768]{1,0:T(8,128)(2,1)S(1)} %copy-done.65, bf16[512,768]{1,0:T(8,128)(2,1)S(1)} %copy-done.67, bf16[512,768]{1,0:T(8,128)(2,1)S(1)} %copy-done.69, ...), custom_call_target="tpu_custom_call" | custom-call | flops 8053063680 | bytes 5505024 | tf_op jit(solution)/shard_map/pallas_call | solution.py:101
  290.9 7.0 %shard_map.262 = (bf16[512,768]{1,0:T(8,128)(2,1)}, f32[1,768]{1,0:T(1,128)S(1)}) custom-call(bf16[512,768]{1,0:T(8,128)(2,1)S(1)} %copy-done.18, bf16[512,768]{1,0:T(8,128)(2,1)S(1)} %copy-done.20, bf16[512,768]{1,0:T(8,128)(2,1)S(1)} %copy-done.22, bf16[512,768]{1,0:T(8,128)(2,1)S(1)} %copy-done.3, f32[512,768]{1,0:T(8,128)S(1)} %copy-done.5, ...), custom_call_target="tpu_custom_call" | custom-call | flops 1811939328 | bytes 9830400 | tf_op jit(solution)/shard_map/pallas_call | solution.py:101
  302.9 9.1 %collective-permute-done.46 = bf16[8,4,3,8,256]{4,3,2,1,0:T(8,128)(2,1)} collective-permute-done((bf16[8,4,3,8,256]{4,3,2,1,0:T(8,128)(2,1)}, bf16[8,4,3,8,256]{4,3,2,1,0:T(8,128)(2,1)}, u32[]{:S(2)}, u32[]{:S(2)}) %collective-permute-start.46) | collective-permute-done | bytes 393248 | tf_op jit(solution)/shard_map/ppermute | solution.py:448
  316.6 9.5 %collective-permute-done.43 = bf16[8,5,3,8,256]{4,3,2,1,0:T(8,128)(2,1)S(1)} collective-permute-done((bf16[8,5,3,8,256]{4,3,2,1,0:T(8,128)(2,1)S(1)}, bf16[8,5,3,8,256]{4,3,2,1,0:T(8,128)(2,1)S(1)}, u32[]{:S(2)}, u32[]{:S(2)}) %collective-permute-start.43) | collective-permute-done | bytes 491552 | tf_op jit(solution)/shard_map/ppermute | solution.py:448
  333.6 12.5 %collective-permute-done.44 = bf16[4,5,3,8,256]{4,3,2,1,0:T(8,128)(2,1)S(1)} collective-permute-done((bf16[4,5,3,8,256]{4,3,2,1,0:T(8,128)(2,1)S(1)}, bf16[4,5,3,8,256]{4,3,2,1,0:T(8,128)(2,1)S(1)}, u32[]{:S(2)}, u32[]{:S(2)}) %collective-permute-start.44) | collective-permute-done | bytes 245792 | tf_op jit(solution)/shard_map/ppermute | solution.py:448
  357.4 6.6 %collective-permute-done.52 = bf16[4,8,3,8,256]{4,3,2,1,0:T(8,128)(2,1)S(1)} collective-permute-done((bf16[4,8,3,8,256]{4,3,2,1,0:T(8,128)(2,1)S(1)}, bf16[4,8,3,8,256]{4,3,2,1,0:T(8,128)(2,1)S(1)}, u32[]{:S(2)}, u32[]{:S(2)}) %collective-permute-start.52) | collective-permute-done | bytes 393248 | tf_op jit(solution)/shard_map/ppermute | solution.py:448
  390.8 7.7 %collective-permute-done.63 = bf16[4,12,3,8,256]{4,3,2,1,0:T(8,128)(2,1)} collective-permute-done((bf16[4,12,3,8,256]{4,3,2,1,0:T(8,128)(2,1)}, bf16[4,12,3,8,256]{4,3,2,1,0:T(8,128)(2,1)}, u32[]{:S(2)}, u32[]{:S(2)}) %collective-permute-start.63) | collective-permute-done | bytes 589856 | tf_op jit(solution)/shard_map/ppermute | solution.py:448
  402.7 10.9 %collective-permute-done.64 = bf16[2,24,3,8,256]{4,3,2,1,0:T(8,128)(2,1)S(1)} collective-permute-done((bf16[2,24,3,8,256]{4,3,2,1,0:T(8,128)(2,1)S(1)}, bf16[2,24,3,8,256]{4,3,2,1,0:T(8,128)(2,1)S(1)}, u32[]{:S(2)}, u32[]{:S(2)}) %collective-permute-start.64) | collective-permute-done | bytes 589856 | tf_op jit(solution)/shard_map/ppermute | solution.py:448
  413.7 5.8 %collective-permute-start.65 = (bf16[24,3,8,256]{3,2,1,0:T(8,128)(2,1)S(1)}, bf16[24,3,8,256]{3,2,1,0:T(8,128)(2,1)S(1)}, u32[]{:S(2)}, u32[]{:S(2)}) collective-permute-start(bf16[24,3,8,256]{3,2,1,0:T(8,128)(2,1)S(1)} %fusion.25), channel_id=1, source_target_pairs={{0,24},{1,25},{2,26},{3,27},{4,28},{5,29},{6,30},{7,31},{8,16},{9,... | collective-permute-start | bytes 884744 | tf_op jit(solution)/shard_map/ppermute | solution.py:448
  (450 shorter events, 203.0 us)
Async XLA Ops:
  40.9 27.4 %collective-permute-start.6 = (bf16[2,25,3,8,256]{4,3,2,1,0:T(8,128)(2,1)S(1)}, bf16[2,25,3,8,256]{4,3,2,1,0:T(8,128)(2,1)S(1)}, u32[]{:S(2)}, u32[]{:S(2)}) collective-permute-start(bf16[2,25,3,8,256]{4,3,2,1,0:T(8,128)(2,1)S(1)} %collective-permute-done.1.refs_1_), channel_id=1, source_target_pairs={{0,2},{1,3},{2,0},{3,1},{4,6},{5,7},{6,4},{7,5},{8,10},{9,11},{10,... | collective-permute-start | bytes 1843208 | tf_op jit(solution)/shard_map/ppermute | solution.py:448
  45.9 23.3 %collective-permute-start.7 = (bf16[2,25,3,8,256]{4,3,2,1,0:T(8,128)(2,1)S(1)}, bf16[2,25,3,8,256]{4,3,2,1,0:T(8,128)(2,1)S(1)}, u32[]{:S(2)}, u32[]{:S(2)}) collective-permute-start(bf16[2,25,3,8,256]{4,3,2,1,0:T(8,128)(2,1)S(1)} %collective-permute-done.2.refs_2_), channel_id=1, source_target_pairs={{0,2},{1,3},{2,0},{3,1},{4,6},{5,7},{6,4},{7,5},{8,10},{9,11},{10,... | collective-permute-start | bytes 1843208 | tf_op jit(solution)/shard_map/ppermute | solution.py:448
  54.6 22.9 %collective-permute-start.22 = (bf16[2,24,3,8,256]{4,3,2,1,0:T(8,128)(2,1)S(1)}, bf16[2,24,3,8,256]{4,3,2,1,0:T(8,128)(2,1)}, u32[]{:S(2)}, u32[]{:S(2)}) collective-permute-start(bf16[2,24,3,8,256]{4,3,2,1,0:T(8,128)(2,1)S(1)} %pad_maximum_fusion.3.refs_0_), channel_id=1, source_target_pairs={{0,1},{1,0},{2,3},{3,2},{4,5},{5,4},{6,7},{7,6},{8,9},{9,8},{10,11... | collective-permute-start | bytes 1769480 | tf_op jit(solution)/shard_map/ppermute | solution.py:448
  68.3 18.6 %collective-permute-start.23 = (bf16[2,24,3,8,256]{4,3,2,1,0:T(8,128)(2,1)S(1)}, bf16[2,24,3,8,256]{4,3,2,1,0:T(8,128)(2,1)S(1)}, u32[]{:S(2)}, u32[]{:S(2)}) collective-permute-start(bf16[2,24,3,8,256]{4,3,2,1,0:T(8,128)(2,1)S(1)} %pad_maximum_fusion.3.refs_0_), channel_id=1, source_target_pairs={{0,4},{1,5},{2,6},{3,7},{4,0},{5,1},{6,2},{7,3},{8,12},{9,13},{10,... | collective-permute-start | bytes 1769480 | tf_op jit(solution)/shard_map/ppermute | solution.py:448
  88.5 50.7 %collective-permute-start.33 = (bf16[2,24,3,8,256]{4,3,2,1,0:T(8,128)(2,1)S(1)}, bf16[2,24,3,8,256]{4,3,2,1,0:T(8,128)(2,1)}, u32[]{:S(2)}, u32[]{:S(2)}) collective-permute-start(bf16[2,24,3,8,256]{4,3,2,1,0:T(8,128)(2,1)S(1)} %pad_maximum_fusion.4.refs_10_), channel_id=1, source_target_pairs={{0,1},{1,0},{2,3},{3,2},{4,5},{5,4},{6,7},{7,6},{8,9},{9,8},{10,11... | collective-permute-start | bytes 1769480 | tf_op jit(solution)/shard_map/ppermute | solution.py:448
  89.9 49.3 %collective-permute-start.34 = (bf16[2,24,3,8,256]{4,3,2,1,0:T(8,128)(2,1)S(1)}, bf16[2,24,3,8,256]{4,3,2,1,0:T(8,128)(2,1)}, u32[]{:S(2)}, u32[]{:S(2)}) collective-permute-start(bf16[2,24,3,8,256]{4,3,2,1,0:T(8,128)(2,1)S(1)} %pad_maximum_fusion.4.refs_10_), channel_id=1, source_target_pairs={{0,4},{1,5},{2,6},{3,7},{4,0},{5,1},{6,2},{7,3},{8,12},{9,13},{10,... | collective-permute-start | bytes 1769480 | tf_op jit(solution)/shard_map/ppermute | solution.py:448
  98.2 51.4 %collective-permute-start.26 = (bf16[2,24,3,8,256]{4,3,2,1,0:T(8,128)(2,1)S(1)}, bf16[2,24,3,8,256]{4,3,2,1,0:T(8,128)(2,1)}, u32[]{:S(2)}, u32[]{:S(2)}) collective-permute-start(bf16[2,24,3,8,256]{4,3,2,1,0:T(8,128)(2,1)S(1)} %pad_maximum_fusion.3.refs_0_), channel_id=1, source_target_pairs={{0,2},{1,3},{2,0},{3,1},{4,6},{5,7},{6,4},{7,5},{8,10},{9,11},{10,... | collective-permute-start | bytes 1769480 | tf_op jit(solution)/shard_map/ppermute | solution.py:448
  111.8 39.7 %collective-permute-start.37 = (bf16[2,24,3,8,256]{4,3,2,1,0:T(8,128)(2,1)S(1)}, bf16[2,24,3,8,256]{4,3,2,1,0:T(8,128)(2,1)}, u32[]{:S(2)}, u32[]{:S(2)}) collective-permute-start(bf16[2,24,3,8,256]{4,3,2,1,0:T(8,128)(2,1)S(1)} %pad_maximum_fusion.4.refs_10_), channel_id=1, source_target_pairs={{0,2},{1,3},{2,0},{3,1},{4,6},{5,7},{6,4},{7,5},{8,10},{9,11},{10,... | collective-permute-start | bytes 1769480 | tf_op jit(solution)/shard_map/ppermute | solution.py:448
  111.8 39.7 %collective-permute-start.27 = (bf16[2,24,3,8,256]{4,3,2,1,0:T(8,128)(2,1)}, bf16[2,24,3,8,256]{4,3,2,1,0:T(8,128)(2,1)}, u32[]{:S(2)}, u32[]{:S(2)}) collective-permute-start(bf16[2,24,3,8,256]{4,3,2,1,0:T(8,128)(2,1)} %collective-permute-done.22.refs_1_), channel_id=1, source_target_pairs={{0,2},{1,3},{2,0},{3,1},{4,6},{5,7},{6,4},{7,5},{8,10},{9,11},{10,... | collective-permute-start | bytes 1769480 | tf_op jit(solution)/shard_map/ppermute | solution.py:448
  149.6 37.7 %collective-permute-start.28 = (bf16[2,24,3,8,256]{4,3,2,1,0:T(8,128)(2,1)S(1)}, bf16[2,24,3,8,256]{4,3,2,1,0:T(8,128)(2,1)S(1)}, u32[]{:S(2)}, u32[]{:S(2)}) collective-permute-start(bf16[2,24,3,8,256]{4,3,2,1,0:T(8,128)(2,1)S(1)} %copy-done.16), channel_id=1, source_target_pairs={{0,2},{1,3},{2,0},{3,1},{4,6},{5,7},{6,4},{7,5},{8,10},{9,11},{10,... | collective-permute-start | bytes 1769480 | tf_op jit(solution)/shard_map/ppermute | solution.py:448
  149.8 20.6 %collective-permute-start.35 = (bf16[2,12,3,8,256]{4,3,2,1,0:T(8,128)(2,1)S(1)}, bf16[2,12,3,8,256]{4,3,2,1,0:T(8,128)(2,1)S(1)}, u32[]{:S(2)}, u32[]{:S(2)}) collective-permute-start(bf16[2,12,3,8,256]{4,3,2,1,0:T(8,128)(2,1)S(1)} %slice.405), channel_id=1, source_target_pairs={{0,4},{1,5},{2,6},{3,7},{4,0},{5,1},{6,2},{7,3},{8,12},{9,13},{10,... | collective-permute-start | bytes 884744 | tf_op jit(solution)/shard_map/ppermute | solution.py:448
  150.3 20.1 %collective-permute-start.36 = (bf16[2,12,3,8,256]{4,3,2,1,0:T(8,128)(2,1)S(1)}, bf16[2,12,3,8,256]{4,3,2,1,0:T(8,128)(2,1)S(1)}, u32[]{:S(2)}, u32[]{:S(2)}) collective-permute-start(bf16[2,12,3,8,256]{4,3,2,1,0:T(8,128)(2,1)S(1)} %slice.406), channel_id=1, source_target_pairs={{0,1},{1,0},{2,3},{3,2},{4,5},{5,4},{6,7},{7,6},{8,9},{9,8},{10,11... | collective-permute-start | bytes 884744 | tf_op jit(solution)/shard_map/ppermute | solution.py:448
  151.5 35.8 %collective-permute-start.38 = (bf16[2,24,3,8,256]{4,3,2,1,0:T(8,128)(2,1)}, bf16[2,24,3,8,256]{4,3,2,1,0:T(8,128)(2,1)S(1)}, u32[]{:S(2)}, u32[]{:S(2)}) collective-permute-start(bf16[2,24,3,8,256]{4,3,2,1,0:T(8,128)(2,1)} %collective-permute-done.33.refs_11_), channel_id=1, source_target_pairs={{0,2},{1,3},{2,0},{3,1},{4,6},{5,7},{6,4},{7,5},{8,10},{9,11},{10,... | collective-permute-start | bytes 1769480 | tf_op jit(solution)/shard_map/ppermute | solution.py:448
  151.5 35.8 %collective-permute-start.39 = (bf16[2,24,3,8,256]{4,3,2,1,0:T(8,128)(2,1)}, bf16[2,24,3,8,256]{4,3,2,1,0:T(8,128)(2,1)S(1)}, u32[]{:S(2)}, u32[]{:S(2)}) collective-permute-start(bf16[2,24,3,8,256]{4,3,2,1,0:T(8,128)(2,1)} %collective-permute-done.34.refs_12_), channel_id=1, source_target_pairs={{0,2},{1,3},{2,0},{3,1},{4,6},{5,7},{6,4},{7,5},{8,10},{9,11},{10,... | collective-permute-start | bytes 1769480 | tf_op jit(solution)/shard_map/ppermute | solution.py:448
  287.0 27.8 %collective-permute-start.53 = (bf16[16,7,3,8,256]{4,3,2,1,0:T(8,128)(2,1)}, bf16[16,7,3,8,256]{4,3,2,1,0:T(8,128)(2,1)}, u32[]{:S(2)}, u32[]{:S(2)}) collective-permute-start(bf16[16,7,3,8,256]{4,3,2,1,0:T(8,128)(2,1)} %get-tuple-element.113), channel_id=1, source_target_pairs={{0,2},{1,3},{2,0},{3,1},{4,6},{5,7},{6,4},{7,5},{8,10},{9,11},{10,... | collective-permute-start | bytes 4128776 | tf_op jit(solution)/shard_map/ppermute | solution.py:448
  287.1 40.9 %collective-permute-start.50 = (bf16[16,8,3,8,256]{4,3,2,1,0:T(8,128)(2,1)}, bf16[16,8,3,8,256]{4,3,2,1,0:T(8,128)(2,1)}, u32[]{:S(2)}, u32[]{:S(2)}) collective-permute-start(bf16[16,8,3,8,256]{4,3,2,1,0:T(8,128)(2,1)} %get-tuple-element.111), channel_id=1, source_target_pairs={{0,2},{1,3},{2,0},{3,1},{4,6},{5,7},{6,4},{7,5},{8,10},{9,11},{10,... | collective-permute-start | bytes 4718600 | tf_op jit(solution)/shard_map/ppermute | solution.py:448
  298.0 54.3 %collective-permute-start.61 = (bf16[16,12,3,8,256]{4,3,2,1,0:T(8,128)(2,1)}, bf16[16,12,3,8,256]{4,3,2,1,0:T(8,128)(2,1)}, u32[]{:S(2)}, u32[]{:S(2)}) collective-permute-start(bf16[16,12,3,8,256]{4,3,2,1,0:T(8,128)(2,1)} %get-tuple-element.117), channel_id=1, source_target_pairs={{0,2},{1,3},{2,0},{3,1},{4,6},{5,7},{6,4},{7,5},{8,10},{9,11},{10,... | collective-permute-start | bytes 7077896 | tf_op jit(solution)/shard_map/ppermute | solution.py:448
  301.6 65.4 %collective-permute-start.58 = (bf16[16,12,3,8,256]{4,3,2,1,0:T(8,128)(2,1)}, bf16[16,12,3,8,256]{4,3,2,1,0:T(8,128)(2,1)S(1)}, u32[]{:S(2)}, u32[]{:S(2)}) collective-permute-start(bf16[16,12,3,8,256]{4,3,2,1,0:T(8,128)(2,1)} %get-tuple-element.115), channel_id=1, source_target_pairs={{0,2},{1,3},{2,0},{3,1},{4,6},{5,7},{6,4},{7,5},{8,10},{9,11},{10,... | collective-permute-start | bytes 7077896 | tf_op jit(solution)/shard_map/ppermute | solution.py:448
  326.1 21.5 %collective-permute-start.54 = (bf16[8,7,3,8,256]{4,3,2,1,0:T(8,128)(2,1)S(1)}, bf16[8,7,3,8,256]{4,3,2,1,0:T(8,128)(2,1)S(1)}, u32[]{:S(2)}, u32[]{:S(2)}) collective-permute-start(bf16[8,7,3,8,256]{4,3,2,1,0:T(8,128)(2,1)S(1)} %add_convert_fusion.3), channel_id=1, source_target_pairs={{0,1},{1,0},{2,3},{3,2},{4,5},{5,4},{6,7},{7,6},{8,9},{9,8},{10,11... | collective-permute-start | bytes 2064392 | tf_op jit(solution)/shard_map/ppermute | solution.py:448
  328.0 18.1 %collective-permute-start.44 = (bf16[4,5,3,8,256]{4,3,2,1,0:T(8,128)(2,1)S(1)}, bf16[4,5,3,8,256]{4,3,2,1,0:T(8,128)(2,1)S(1)}, u32[]{:S(2)}, u32[]{:S(2)}) collective-permute-start(bf16[4,5,3,8,256]{4,3,2,1,0:T(8,128)(2,1)S(1)} %add_convert_fusion.10), channel_id=1, source_target_pairs={{0,1},{1,0},{2,3},{3,2},{4,5},{5,4},{6,7},{7,6},{8,9},{9,8},{10,11... | collective-permute-start | bytes 737288 | tf_op jit(solution)/shard_map/ppermute | solution.py:448
  330.6 20.1 %collective-permute-start.51 = (bf16[8,8,3,8,256]{4,3,2,1,0:T(8,128)(2,1)S(1)}, bf16[8,8,3,8,256]{4,3,2,1,0:T(8,128)(2,1)S(1)}, u32[]{:S(2)}, u32[]{:S(2)}) collective-permute-start(bf16[8,8,3,8,256]{4,3,2,1,0:T(8,128)(2,1)S(1)} %add_convert_fusion.2), channel_id=1, source_target_pairs={{0,4},{1,5},{2,6},{3,7},{4,0},{5,1},{6,2},{7,3},{8,12},{9,13},{10,... | collective-permute-start | bytes 2359304 | tf_op jit(solution)/shard_map/ppermute | solution.py:448
  347.2 20.5 %collective-permute-start.48 = (bf16[2,9,3,8,256]{4,3,2,1,0:T(8,128)(2,1)S(1)}, bf16[2,9,3,8,256]{4,3,2,1,0:T(8,128)(2,1)S(1)}, u32[]{:S(2)}, u32[]{:S(2)}) collective-permute-start(bf16[2,9,3,8,256]{4,3,2,1,0:T(8,128)(2,1)S(1)} %fusion.14), channel_id=1, source_target_pairs={{0,8},{1,9},{2,10},{3,11},{4,12},{5,13},{6,14},{7,15},{8,0},{9,1},... | collective-permute-start | bytes 663560 | tf_op jit(solution)/shard_map/ppermute | solution.py:448
  353.9 30.2 %collective-permute-start.62 = (bf16[8,12,3,8,256]{4,3,2,1,0:T(8,128)(2,1)S(1)}, bf16[8,12,3,8,256]{4,3,2,1,0:T(8,128)(2,1)S(1)}, u32[]{:S(2)}, u32[]{:S(2)}) collective-permute-start(bf16[8,12,3,8,256]{4,3,2,1,0:T(8,128)(2,1)S(1)} %add_convert_fusion), channel_id=1, source_target_pairs={{0,1},{1,0},{2,3},{3,2},{4,5},{5,4},{6,7},{7,6},{8,9},{9,8},{10,11... | collective-permute-start | bytes 3538952 | tf_op jit(solution)/shard_map/ppermute | solution.py:448
  367.3 19.7 %collective-permute-start.59 = (bf16[8,12,3,8,256]{4,3,2,1,0:T(8,128)(2,1)S(1)}, bf16[8,12,3,8,256]{4,3,2,1,0:T(8,128)(2,1)S(1)}, u32[]{:S(2)}, u32[]{:S(2)}) collective-permute-start(bf16[8,12,3,8,256]{4,3,2,1,0:T(8,128)(2,1)S(1)} %add_convert_fusion.1), channel_id=1, source_target_pairs={{0,4},{1,5},{2,6},{3,7},{4,0},{5,1},{6,2},{7,3},{8,12},{9,13},{10,... | collective-permute-start | bytes 3538952 | tf_op jit(solution)/shard_map/ppermute | solution.py:448
  (147 other events, 1670.0 us)
